TPU v7x, 32 devices: a whole 2x2x4 slice. The times are simulated.
32 devices in a mesh: bank: 8 (over z, y), tp: 4 (over x, core).
Axes of the slice: x: 2, y: 2, z: 4, core: 2. Of those that a mesh axis runs over, the one named last changes fastest.
Arguments:
- hidden: bfloat16 [16, 512, 14336], P('bank', None, 'tp'), may hold values from -6 to 6
- out_grad: bfloat16 [16, 512, 4096], P('bank', None, 'tp'), may hold values from -6 to 6
- proj_in: bfloat16 [64, 14336], P(None, 'tp'), may hold values from -0.046875 to 0.046875
- proj_out: bfloat16 [64, 4096], P(None, 'tp'), may hold values from -0.09375 to 0.09375
- lengths: int32 [16], P('bank'), may hold values from 1 to 512, 6144 in all
- pair_perm: int32 [16], replicated, may hold values from 0 to 15, each once
- bank_slab: bfloat16 [8192, 4096], P('bank', 'tp'), may hold values from -6 to 6
Outputs:
- scores: float32 [8, 8192], P('tp', 'bank')
Inputs may be any that keep to these rules, and one draw needn't show every extreme that they name: pair_perm holds every variant index exactly once. `lengths`: some prompt fills all 512 slots.
All inputs are finite; a program needn't handle non-finite values. No bound on the sum of `lengths` on one device may be relied on, other than what follows from the above.
Results may differ from a plain program's by a relative error of at most 0.0029.
Values sent between devices are 32-bit elements; how exact they have to be, the bound alone decides.
No kernel may reach another device: no remote copies, remote signals or barrier semaphores. Data moves between devices by JAX's collectives and lax.ppermute only.
A program may use at most 64 MiB of HBM per device.

v0:
```python
import jax
import jax.numpy as jnp
from jax import lax
from jax.sharding import PartitionSpec as P

epsilon = 1e-06


def per_device(hidden, out_grad, proj_in, proj_out, lengths, pair_perm, bank_slab):
    ex_dev, seq_len, ff_dev = hidden.shape
    factor_rank = proj_in.shape[0]
    tp_count = lax.axis_size("tp")
    share_rows = factor_rank // tp_count
    tok_rows = hidden.reshape(ex_dev * seq_len, ff_dev)
    grad_rows = out_grad.reshape(ex_dev * seq_len, out_grad.shape[2])
    in_part = jnp.einsum("rf,tf->rt", proj_in, tok_rows, preferred_element_type=jnp.float32)
    out_part = jnp.einsum("rd,td->rt", proj_out, grad_rows, preferred_element_type=jnp.float32)
    in_all, out_all = lax.psum((in_part, out_part), "tp")
    in_mine = lax.dynamic_slice_in_dim(in_all, lax.axis_index("tp") * share_rows, share_rows, 0)
    positions = jnp.arange(seq_len, dtype=jnp.int32)
    live_mask = (positions[None, :] < lengths[:, None]).astype(jnp.float32)
    in_three = in_mine.reshape(share_rows, ex_dev, seq_len) * live_mask[None, :, :]
    out_three = out_all.reshape(factor_rank, ex_dev, seq_len)
    grads = jnp.einsum("ies,jes->eij", in_three, out_three, precision=lax.Precision.HIGHEST)
    grads = grads.reshape(ex_dev, share_rows * factor_rank)
    benign = pair_perm[0::2]
    harmful = pair_perm[1::2]
    all_grads = lax.all_gather(grads, "bank", axis=0, tiled=True)
    example_ids = jnp.arange(all_grads.shape[0], dtype=jnp.int32)
    pair_signs = (example_ids[None, :] == harmful[:, None]).astype(jnp.float32) - (
        example_ids[None, :] == benign[:, None]
    ).astype(jnp.float32)
    queries = jnp.dot(pair_signs, all_grads, precision=lax.Precision.HIGHEST)
    query_part = jnp.sum(queries * queries, axis=1)
    slab_wide = bank_slab.astype(jnp.float32)
    bank_part = jnp.sum(slab_wide * slab_wide, axis=1)
    query_sq, bank_sq = lax.psum((query_part, bank_part), "tp")
    query_low = queries.astype(jnp.bfloat16)
    pair_count = queries.shape[0]
    pairs_mine = pair_count // tp_count
    dots = lax.psum_scatter(
        lax.dot_general(
            query_low, bank_slab, (((1,), (1,)), ((), ())), preferred_element_type=jnp.float32
        ),
        "tp",
        scatter_dimension=0,
        tiled=True,
    )
    query_mine = lax.dynamic_slice_in_dim(
        query_sq, lax.axis_index("tp") * pairs_mine, pairs_mine, 0
    )
    return (
        dots
        * factor_rank
        * lax.rsqrt(query_mine + epsilon)[:, None]
        * lax.rsqrt(bank_sq + epsilon)[None, :]
    )


def solution(mesh):
    return jax.shard_map(
        per_device,
        mesh=mesh,
        in_specs=(
            P("bank", None, "tp"),
            P("bank", None, "tp"),
            P(None, "tp"),
            P(None, "tp"),
            P("bank"),
            P(),
            P("bank", "tp"),
        ),
        out_specs=P("tp", "bank"),
        check_vma=False,
    )
```

profile of v0, /device:TPU:0, one launch (start us, length us, event | category | flops | bytes accessed | tf_op | source)
XLA Modules:
  0.0 106.7 jit_solution(6092086413698578834)
XLA Ops:
  6.5 0.0 copy-start
  6.5 0.0 copy-start.1
  6.5 0.0 all-reduce.5.cloned.1.call-start
  6.5 1.6 %copy-done = bf16[2,512,1024]{2,1,0:T(8,128)(2,1)S(1)} copy-done((bf16[2,512,1024]{2,1,0:T(8,128)(2,1)S(1)}, bf16[2,512,1024]{2,1,0:T(8,128)(2,1)}, u32[]{:S(2)}) %copy-start) | copy-done | bytes 2097176
  8.1 1.7 %fusion.12 = f32[64,1024]{1,0:T(8,128)S(1)} fusion(bf16[64,1024]{1,0:T(8,128)(2,1)} %param.10, bf16[1024,1024]{1,0:T(8,128)(2,1)S(1)} %bitcast.18), kind=kOutput, calls=%fused_computation.23 | convolution fusion | flops 134217728 | bytes 2490368 | tf_op jit(solution)/shard_map/rd,td->rt/dot_general | solution.py:17
  9.8 0.7 copy.17
  10.5 0.0 copy-done.1
  10.5 0.0 copy-start.2
  10.5 0.0 copy-start.3
  10.5 0.0 copy-start.4
  10.5 6.1 %fusion.11 = f32[64,1024]{1,0:T(8,128)} fusion(bf16[64,3584]{1,0:T(8,128)(2,1)S(1)} %copy-done.1, bf16[1024,3584]{1,0:T(8,128)(2,1)} %bitcast.19), kind=kOutput, calls=%fused_computation.22 | convolution fusion | flops 469762048 | bytes 8060928 | tf_op jit(solution)/shard_map/rf,tf->rt/dot_general | solution.py:16
  16.7 0.0 all-reduce.5.cloned.1.call-update
  16.7 0.0 copy-done.2
  16.7 0.1 compare_convert_fusion
  16.8 0.0 copy-done.3
  16.8 0.1 slice.7
  16.9 0.1 slice.6
  17.0 0.0 copy-done.4
  17.0 0.6 dynamic-slice
  18.2 2.1 %multiply_reduce_fusion = f32[1024]{0:T(1024)S(1)} fusion(bf16[1024,1024]{1,0:T(8,128)(2,1)} %param.13), kind=kLoop, calls=%fused_computation | loop fusion | flops 3144704 | bytes 2101248 | tf_op jit(solution)/shard_map/reduce_sum | solution.py:36
  20.3 32.5 %all-reduce.5.cloned.1.call-done = (f32[64,2,512]{2,0,1:T(8,128)}, f32[64,1024]{1,0:T(8,128)}) async-done(((f32[64,2,512]{2,0,1:T(8,128)}, f32[64,1024]{1,0:T(8,128)}), (f32[64,2,512]{2,0,1:T(8,128)}, f32[64,1024]{1,0:T(8,128)})) %all-reduce.5.cloned.1.call-update) | async-done | bytes 524304 | tf_op jit(solution)/shard_map/psum | solution.py:18
  52.7 0.8 constant_dynamic-slice_fusion
  53.6 0.1 reshape.39
  53.7 1.3 %fusion = f32[2,16,64]{2,1,0:T(8,128)S(1)} fusion(f32[64,2,512]{2,0,1:T(8,128)} %get-tuple-element.8, f32[16,2,512]{2,1,0:T(2,128)S(1)} %bitcast.23), kind=kOutput, calls=%fused_computation.2 | convolution fusion | flops 12582912 | bytes 335872 | tf_op jit(solution)/shard_map/ies,jes->eij/dot_general | solution.py:24
  54.9 0.1 reshape.43
  55.0 30.6 %all-gather = f32[8,2,1024]{2,1,0:T(2,128)S(1)} all-gather(f32[1,2,1024]{2,1,0:T(2,128)S(1)} %reshape.43), channel_id=1, replica_groups=mesh['bank'=8,'tp'=4] {'bank'}, dimensions={0}, use_global_device_ids=true | all-gather | bytes 73728 | tf_op jit(solution)/shard_map/all_gather | solution.py:28
  85.6 0.3 multiply_reduce_fusion.1
  86.0 2.2 %fusion.2 = f32[8,1024]{1,0:T(8,128)S(1)} fusion(bf16[1024,1024]{1,0:T(8,128)(2,1)} %param.13, bf16[8,1024]{1,0:T(8,128)(2,1)S(1)} %get-tuple-element.11), kind=kOutput, calls=%fused_computation.6 | convolution fusion | flops 16777216 | bytes 2146304 | tf_op jit(solution)/shard_map/dot_general | solution.py:42
  88.2 10.9 %all-reduce.1 = (f32[8,1024]{1,0:T(8,128)S(1)}, f32[8]{0:T(128)S(1)}, f32[1024]{0:T(1024)S(1)}) all-reduce(f32[8,1024]{1,0:T(8,128)S(1)} %fusion.2, f32[8]{0:T(128)S(1)} %get-tuple-element.10, f32[1024]{0:T(1024)S(1)} %multiply_reduce_fusion), channel_id=2, replica_groups=mesh['bank'=8,'tp'=4] {'tp'}, use_global_device_ids=true, to_apply=%region_2.0.clone | all-reduce | flops 9224 | bytes 73792
  99.1 0.1 rsqrt_multiply_fusion
  99.2 0.7 fusion.4
  (4 shorter events, 0.1 us)
Async XLA Ops:
  6.5 1.6 %copy-start = (bf16[2,512,1024]{2,1,0:T(8,128)(2,1)S(1)}, bf16[2,512,1024]{2,1,0:T(8,128)(2,1)}, u32[]{:S(2)}) copy-start(bf16[2,512,1024]{2,1,0:T(8,128)(2,1)} %param.8) | copy-start | bytes 6291460
  6.5 4.0 %copy-start.1 = (bf16[64,3584]{1,0:T(8,128)(2,1)S(1)}, bf16[64,3584]{1,0:T(8,128)(2,1)}, u32[]{:S(2)}) copy-start(bf16[64,3584]{1,0:T(8,128)(2,1)} %param.9) | copy-start | bytes 1376260
  6.5 46.2 %all-reduce.5.cloned.1.call-start = ((), (), s32[]{:S(2)}) async-start(), calls=%async_computation | async-start | bytes 1048576 | tf_op jit(solution)/shard_map/psum | solution.py:18
  10.5 6.2 %copy-start.2 = (s32[2]{0:T(128)S(1)}, s32[2]{0:T(128)}, u32[]{:S(2)}) copy-start(s32[2]{0:T(128)} %param.11) | copy-start | bytes 28
  10.5 6.3 %copy-start.3 = (s32[16]{0:T(128)S(1)}, s32[16]{0:T(128)}, u32[]{:S(2)}) copy-start(s32[16]{0:T(128)} %param.12) | copy-start | bytes 196
  10.5 6.5 %copy-start.4 = (u32[32]{0:T(128)S(1)}, u32[32]{0:T(128)}, u32[]{:S(2)}) copy-start(u32[32]{0:T(128)} %constant.26) | copy-start | bytes 388
Sparse Core Ops, SparseCore 0:
  16.8 35.8 all-reduce.4
where the time goes:
time: 107 us
  blocking collectives  41.4 us (39%)
  waiting for transfers between devices  32.5 us (30%)
  between operations  14.1 us (13%)
  matrix products  11.7 us (11%)
  local copies, waits for them, and re-layouts  4.14 us (4%)
  other arithmetic  2.91 us (3%)
    psum x1, waiting for transfers between devices, per_device(): in_all, out_all = lax.psum((in_part, out_part), 'tp')  32.5 us
    all_gather x1, blocking collectives, per_device(): all_grads = lax.all_gather(grads, 'bank', axis=0, tiled=True)  30.6 us
    unnamed x1, blocking collectives  10.9 us
    dot_general x1, matrix products, per_device(): jnp.einsum('rf,tf->rt', proj_in, tok_rows, preferred_element_type=jnp.flo...  6.14 us
    unnamed x14, local copies, waits for them, and re-layouts  2.33 us
    dot_general x1, matrix products, per_device(): lax.dot_general(query_low, bank_slab, (((1,), (1,)), ((), ())), preferred...  2.24 us
  transfers between devices with their start and end apart: 1, of which 1 were waited for; matrix products, arithmetic and copies ran while one was open for 3% of the time, Pallas kernels for 0%

commit v1 on v0

v1 whole, which is shorter than its diff:
```python
import jax
import jax.numpy as jnp
from jax import lax
from jax.sharding import PartitionSpec as P

epsilon = 1e-06


def flip(step):
    return [(i, i ^ step) for i in range(4)]


def per_device(hidden, out_grad, proj_in, proj_out, lengths, pair_perm, bank_slab):
    ex_dev, seq_len, _ = hidden.shape
    factor_rank = proj_in.shape[0]
    tp_count = lax.axis_size("tp")
    bank_count = lax.axis_size("bank")
    k = lax.axis_index("tp")
    core = lax.rem(k, 2)
    share_rows = factor_rank // tp_count

    def pick(arr, which):
        return lax.dynamic_index_in_dim(arr, which, 0, keepdims=False)

    def factor(proj, rows):
        return jnp.einsum("rf,tf->rt", proj, rows, preferred_element_type=jnp.float32)

    out_send = factor(proj_out, pick(out_grad, 1 - core))
    out_keep = factor(proj_out, pick(out_grad, core))
    out_chip = out_keep + lax.ppermute(out_send, "tp", flip(1))
    out_full = out_chip + lax.ppermute(out_chip, "tp", flip(2))
    in_send = factor(proj_in, pick(hidden, 1 - core))
    in_keep = factor(proj_in, pick(hidden, core))
    in_chip = in_keep + lax.ppermute(in_send, "tp", flip(1))
    positions = jnp.arange(seq_len, dtype=jnp.int32)
    live_mask = (positions < pick(lengths, core)).astype(jnp.float32)
    grads = jnp.einsum(
        "it,jt->ij", in_chip * live_mask[None, :], out_full, precision=lax.Precision.HIGHEST
    )
    cols = share_rows * factor_rank
    outgoing = jnp.broadcast_to(
        grads.reshape(1, tp_count, cols), (bank_count, tp_count, cols)
    ).reshape(bank_count * tp_count, cols)
    partials = lax.all_to_all(outgoing, ("bank", "tp"), 0, 0, tiled=True)
    source = jnp.arange(bank_count * tp_count, dtype=jnp.int32)
    example_ids = (source // tp_count) * ex_dev + source % 2
    pair_count = pair_perm.shape[0] // 2
    pairs_mine = pair_count // tp_count
    order = jnp.arange(pair_count, dtype=jnp.int32)
    pair_ids = ((order // pairs_mine) ^ k) * pairs_mine + order % pairs_mine
    benign = pair_perm[0::2][pair_ids]
    harmful = pair_perm[1::2][pair_ids]
    pair_signs = (example_ids[None, :] == harmful[:, None]).astype(jnp.float32) - (
        example_ids[None, :] == benign[:, None]
    ).astype(jnp.float32)
    queries = jnp.dot(pair_signs, partials, precision=lax.Precision.HIGHEST)
    query_part = jnp.sum(queries * queries, axis=1)
    slab_wide = bank_slab.astype(jnp.float32)
    bank_part = jnp.sum(slab_wide * slab_wide, axis=1)
    dots = lax.dot_general(
        queries.astype(jnp.bfloat16),
        bank_slab,
        (((1,), (1,)), ((), ())),
        preferred_element_type=jnp.float32,
    )
    rows = bank_slab.shape[0]
    message = jnp.concatenate(
        [
            dots.reshape(tp_count, pairs_mine, rows),
            jnp.broadcast_to(bank_part[None, None, :], (tp_count, 1, rows)),
            jnp.pad(
                query_part.reshape(tp_count, 1, pairs_mine), ((0, 0), (0, 0), (0, rows - pairs_mine))
            ),
        ],
        axis=1,
    )
    total = message[0]
    for step in range(1, 4):
        total = total + lax.ppermute(message[step], "tp", flip(step))
    query_sq = total[pairs_mine + 1, :pairs_mine]
    bank_sq = total[pairs_mine]
    return (
        total[:pairs_mine]
        * factor_rank
        * lax.rsqrt(query_sq + epsilon)[:, None]
        * lax.rsqrt(bank_sq + epsilon)[None, :]
    )


def solution(mesh):
    return jax.shard_map(
        per_device,
        mesh=mesh,
        in_specs=(
            P("bank", None, "tp"),
            P("bank", None, "tp"),
            P(None, "tp"),
            P(None, "tp"),
            P("bank"),
            P(),
            P("bank", "tp"),
        ),
        out_specs=P("tp", "bank"),
        check_vma=False,
    )
```

time: 107 us -> 36.4 us (0.34)
  blocking collectives: 41.4 us -> 0 us
  waiting for transfers between devices: 32.5 us -> 7.19 us
  between operations: 14.1 us -> 0.14 us
  starting transfers between devices: 0.01 us -> 11.7 us
  matrix products: 11.7 us -> 10.5 us
    psum x1 -> x0, waiting for transfers between devices: 32.5 us -> none  [per_device(): in_all, out_all = lax.psum((in_part, out_part), 'tp')]
    all_gather x1 -> x0, blocking collectives: 30.6 us -> none  [per_device(): all_grads = lax.all_gather(grads, 'bank', axis=0, tiled=True)]
    unnamed x1 -> x0, blocking collectives: 10.9 us -> none
    all_to_all x0 -> x1, starting transfers between devices: none -> 6.09 us  [per_device(): partials = lax.all_to_all(outgoing, ('bank', 'tp'), 0, 0, tiled=True)]
    ppermute x0 -> x6, starting transfers between devices: none -> 5.57 us  [the longest x1 3 us: per_device(): out_full = out_chip + lax.ppermute(out_chip, 'tp', flip(2))]
    all_to_all x0 -> x1, waiting for transfers between devices: none -> 4.64 us  [per_device(): partials = lax.all_to_all(outgoing, ('bank', 'tp'), 0, 0, tiled=True)]
    ppermute x0 -> x6, waiting for transfers between devices: none -> 2.55 us  [the longest x3 2.07 us: per_device(): total = total + lax.ppermute(message[step], 'tp', flip(step))]
    unnamed x14 -> x10, local copies, waits for them, and re-layouts: 2.33 us -> 0.02 us
  transfers between devices with their start and end apart: 1 -> 7, of which waited for: 1 -> 4; matrix products, arithmetic and copies ran while one was open for 3% -> 25% of each run, Pallas kernels for 0% -> 0%
where the time goes in v1:
time: 36.4 us; the launch traced here: 36.1 us
  starting transfers between devices  11.7 us (32%)
  matrix products  10.5 us (29%)
  waiting for transfers between devices  7.19 us (20%)
  other arithmetic  3.49 us (10%)
  local copies, waits for them, and re-layouts  3.15 us (9%)
    dot_general x4, matrix products, factor(): jnp.einsum('rf,tf->rt', proj, rows, preferred_element_type=jnp.float32)  7.64 us
    all_to_all x1, starting transfers between devices, per_device(): partials = lax.all_to_all(outgoing, ('bank', 'tp'), 0, 0, tiled=True)  6.09 us
    all_to_all x1, waiting for transfers between devices, per_device(): partials = lax.all_to_all(outgoing, ('bank', 'tp'), 0, 0, tiled=True)  4.64 us
    ppermute x1, starting transfers between devices, per_device(): out_full = out_chip + lax.ppermute(out_chip, 'tp', flip(2))  3 us
    dot_general x1, matrix products, per_device(): lax.dot_general(queries.astype(jnp.bfloat16), bank_slab, (((1,), (1,)), (...  2.24 us
    ppermute x3, waiting for transfers between devices, per_device(): total = total + lax.ppermute(message[step], 'tp', flip(step))  2.07 us
    reduce_sum x1, other arithmetic, per_device(): bank_part = jnp.sum(slab_wide * slab_wide, axis=1)  2.07 us
    ppermute x3, starting transfers between devices, per_device(): total = total + lax.ppermute(message[step], 'tp', flip(step))  1.93 us
  transfers between devices with their start and end apart: 7, of which 4 were waited for; matrix products, arithmetic and copies ran while one was open for 25% of the time, Pallas kernels for 0%

profile of v1, /device:TPU:0, one launch (start us, length us, event | category | flops | bytes accessed | tf_op | source)
XLA Modules:
  0.0 36.1 jit_solution(3115850698064851868)
XLA Ops:
  0.0 0.0 copy-start
  0.0 0.0 copy-start.1
  0.0 0.0 copy-start.3
  0.0 0.0 copy-start.2
  0.0 3.5 %fusion.15 = f32[64,512]{1,0:T(8,128)S(1)} fusion(bf16[64,3584]{1,0:T(8,128)(2,1)} %param.9, bf16[2,512,3584]{2,1,0:T(8,128)(2,1)} %param.7, s32[]{:T(128)S(6)} %select_n.78), kind=kOutput, calls=%fused_computation.12 | convolution fusion | flops 234881024 | bytes 4259844 | tf_op jit(solution)/shard_map/rf,tf->rt/dot_general | solution.py:26
  3.5 0.5 %collective-permute-start = (f32[64,512]{1,0:T(8,128)S(1)}, f32[64,512]{1,0:T(8,128)S(1)}, u32[]{:S(2)}, u32[]{:S(2)}) collective-permute-start(f32[64,512]{1,0:T(8,128)S(1)} %fusion.15), channel_id=1, source_target_pairs={{0,1},{1,0},{2,3},{3,2},{4,5},{5,4},{6,7},{7,6},{8,9},{9,8},{10,11... | collective-permute-start | bytes 393224 | tf_op jit(solution)/shard_map/ppermute | solution.py:34
  4.0 0.0 copy-done
  4.0 0.0 copy-done.1
  4.0 0.4 %convolution_bitcast_fusion = f32[64,512]{1,0:T(8,128)S(1)} fusion(bf16[64,1024]{1,0:T(8,128)(2,1)S(1)} %copy-done.1, bf16[2,512,1024]{2,1,0:T(8,128)(2,1)S(1)} %copy-done, s32[]{:T(128)S(6)} %select_n.78), kind=kOutput, calls=%fused_computation.13 | convolution fusion | flops 67108864 | bytes 1310724 | tf_op jit(solution)/shard_map/rf,tf->rt/dot_general | solution.py:26
  4.5 0.1 collective-permute-start.1
  4.6 0.0 copy-done.3
  4.6 0.6 %dynamic_slice.20 = s32[1]{0:T(128)} dynamic-slice(s32[2]{0:T(128)S(1)} %copy-done.3, s32[]{:T(128)S(6)} %select_n.77), dynamic_slice_sizes={1} | dynamic-slice | bytes 12 | tf_op jit(solution)/shard_map/jit(dynamic_index_in_dim)/dynamic_slice | solution.py:23
  5.2 0.6 %fusion.43 = f32[512]{0:T(512)S(1)} fusion(s32[]{:T(128)} %bitcast.5), kind=kLoop, calls=%fused_computation.52 | loop fusion | flops 1024 | bytes 2052 | tf_op jit(solution)/shard_map/convert_element_type | solution.py:36
  5.9 0.0 collective-permute-done.1
  5.9 0.4 %fusion.18 = f32[64,512]{1,0:T(8,128)S(1)} fusion(f32[64,512]{1,0:T(8,128)S(1)} %collective-permute-done.1, bf16[64,1024]{1,0:T(8,128)(2,1)S(1)} %copy-done.1, bf16[2,512,1024]{2,1,0:T(8,128)(2,1)S(1)} %copy-done, s32[]{:T(128)S(6)} %select_n.77), kind=kOutput, calls=%fused_computation.15 | convolution fusion | flops 67141632 | bytes 1441796 | tf_op jit(solution)/shard_map/rf,tf->rt/dot_general | solution.py:26
  6.3 0.0 copy-start.4
  6.4 3.0 %collective-permute-start.2 = (f32[64,512]{1,0:T(8,128)S(1)}, f32[64,512]{1,0:T(8,128)S(1)}, u32[]{:S(2)}, u32[]{:S(2)}) collective-permute-start(f32[64,512]{1,0:T(8,128)S(1)} %fusion.18), channel_id=1, source_target_pairs={{0,2},{1,3},{2,0},{3,1},{4,6},{5,7},{6,4},{7,5},{8,10},{9,11},{10,... | collective-permute-start | bytes 393224 | tf_op jit(solution)/shard_map/ppermute | solution.py:31
  9.4 0.0 collective-permute-done
  9.4 0.0 copy-done.2
  9.4 3.3 %fusion.12 = f32[64,512]{1,0:T(8,128)S(1)} fusion(f32[64,512]{1,0:T(8,128)S(1)} %collective-permute-done, bf16[64,3584]{1,0:T(8,128)(2,1)S(1)} %copy-done.2, bf16[2,512,3584]{2,1,0:T(8,128)(2,1)} %param.7, s32[]{:T(128)S(6)} %select_n.77, f32[512]{0:T(512)S(1)} %fusion.43), kind=kOutput, calls=%fused_computation.11 | convolution fusion | flops 234946560 | bytes 4392964 | tf_op jit(solution)/shard_map/rf,tf->rt/dot_general | solution.py:26
  12.6 0.4 %collective-permute-done.2 = f32[64,512]{1,0:T(8,128)S(1)} collective-permute-done((f32[64,512]{1,0:T(8,128)S(1)}, f32[64,512]{1,0:T(8,128)S(1)}, u32[]{:S(2)}, u32[]{:S(2)}) %collective-permute-start.2) | collective-permute-done | bytes 131104 | tf_op jit(solution)/shard_map/ppermute | solution.py:31
  13.1 0.3 fusion.26
  13.3 0.1 broadcast_in_dim.6
  13.5 0.8 %all_to_all.8 = f32[32,1,1024]{2,1,0:T(1,128)} reshape(f32[8,4,1024]{2,1,0:T(4,128)S(1)} %broadcast_in_dim.7) | data formatting | bytes 262144 | tf_op jit(solution)/shard_map/all_to_all | solution.py:44
  14.3 6.1 %all-to-all-start = ((f32[32,1,1024]{2,1,0:T(1,128)}), f32[32,1,1024]{2,1,0:T(1,128)S(1)}, u32[]{:S(2)}, u32[]{:S(2)}) async-start(f32[32,1,1024]{2,1,0:T(1,128)} %all_to_all.8), calls=%async_computation | async-start | bytes 262144 | tf_op jit(solution)/shard_map/all_to_all | solution.py:44
  20.4 0.0 copy-done.4
  20.4 0.1 slice.28
  20.5 0.1 slice.27
  20.6 0.7 %gather_fusion.1 = s32[8]{0:T(128)S(1)} fusion(s32[8]{0:T(128)S(1)} %slice.28, s32[1024]{0:T(1024)S(1)} %pad_clamp_fusion), kind=kCustom, calls=%fused_computation.1 | custom fusion | bytes 96 | tf_op jit(solution)/shard_map/gather | solution.py:51
  21.2 0.6 %gather_fusion = s32[8]{0:T(128)S(1)} fusion(s32[8]{0:T(128)S(1)} %slice.27, s32[1024]{0:T(1024)S(1)} %pad_clamp_fusion), kind=kCustom, calls=%fused_computation | custom fusion | bytes 96 | tf_op jit(solution)/shard_map/gather | solution.py:52
  21.9 2.1 %multiply_reduce_fusion = f32[1024]{0:T(1024)S(1)} fusion(bf16[1024,1024]{1,0:T(8,128)(2,1)} %param.13), kind=kLoop, calls=%fused_computation.2 | loop fusion | flops 3144704 | bytes 2101248 | tf_op jit(solution)/shard_map/reduce_sum | solution.py:59
  24.0 4.6 %all-to-all-done = f32[32,1,1024]{2,1,0:T(1,128)S(1)} async-done(((f32[32,1,1024]{2,1,0:T(1,128)}), f32[32,1,1024]{2,1,0:T(1,128)S(1)}, u32[]{:S(2)}, u32[]{:S(2)}) %all-to-all-start) | async-done | bytes 131104 | tf_op jit(solution)/shard_map/all_to_all | solution.py:44
  28.6 0.3 multiply_reduce_fusion.1
  29.0 0.1 reshape.123
  29.0 2.2 %fusion.31 = f32[8,1024]{1,0:T(8,128)S(1)} fusion(bf16[1024,1024]{1,0:T(8,128)(2,1)} %param.13, bf16[8,1024]{1,0:T(8,128)(2,1)S(1)} %get-tuple-element.9), kind=kOutput, calls=%fused_computation.35 | convolution fusion | flops 16777216 | bytes 2146304 | tf_op jit(solution)/shard_map/dot_general | solution.py:60
  31.4 0.2 collective-permute-start.5
  31.6 1.7 %collective-permute-start.4 = (f32[4,1024]{1,0:T(4,128)S(1)}, f32[4,1024]{1,0:T(4,128)S(1)}, u32[]{:S(2)}, u32[]{:S(2)}) collective-permute-start(f32[4,1024]{1,0:T(4,128)S(1)} %get-tuple-element.7), channel_id=1, source_target_pairs={{0,2},{1,3},{2,0},{3,1},{4,6},{5,7},{6,4},{7,5},{8,10},{9,11},{10,... | collective-permute-start | bytes 49160 | tf_op jit(solution)/shard_map/ppermute | solution.py:79
  33.3 0.0 collective-permute-start.3
  33.3 1.3 %collective-permute-done.5 = f32[4,1024]{1,0:T(4,128)S(1)} collective-permute-done((f32[4,1024]{1,0:T(4,128)S(1)}, f32[4,1024]{1,0:T(4,128)S(1)}, u32[]{:S(2)}, u32[]{:S(2)}) %collective-permute-start.5) | collective-permute-done | bytes 16416 | tf_op jit(solution)/shard_map/ppermute | solution.py:79
  34.6 0.8 %collective-permute-done.4 = f32[4,1024]{1,0:T(4,128)S(1)} collective-permute-done((f32[4,1024]{1,0:T(4,128)S(1)}, f32[4,1024]{1,0:T(4,128)S(1)}, u32[]{:S(2)}, u32[]{:S(2)}) %collective-permute-start.4) | collective-permute-done | bytes 16416 | tf_op jit(solution)/shard_map/ppermute | solution.py:79
  35.4 0.0 collective-permute-done.3
  35.5 0.7 %fusion.33 = f32[2,1024]{1,0:T(2,128)} fusion(f32[4,1024]{1,0:T(4,128)S(1)} %fusion.30, f32[2]{0:T(128)S(1)} %fusion.56, f32[1024]{0:T(1024)S(1)} %bitcast.67), kind=kLoop, calls=%fused_computation.38 | loop fusion | flops 4096 | bytes 20488 | tf_op jit(solution)/shard_map/mul | solution.py:83
  (11 shorter events, 0.2 us)
Async XLA Ops:
  0.0 4.0 %copy-start = (bf16[2,512,1024]{2,1,0:T(8,128)(2,1)S(1)}, bf16[2,512,1024]{2,1,0:T(8,128)(2,1)}, u32[]{:S(2)}) copy-start(bf16[2,512,1024]{2,1,0:T(8,128)(2,1)} %param.8) | copy-start | bytes 6291460
  0.0 4.0 %copy-start.1 = (bf16[64,1024]{1,0:T(8,128)(2,1)S(1)}, bf16[64,1024]{1,0:T(8,128)(2,1)}, u32[]{:S(2)}) copy-start(bf16[64,1024]{1,0:T(8,128)(2,1)} %param.10) | copy-start | bytes 393220
  0.0 4.6 %copy-start.3 = (s32[2]{0:T(128)S(1)}, s32[2]{0:T(128)}, u32[]{:S(2)}) copy-start(s32[2]{0:T(128)} %param.11) | copy-start | bytes 28
  0.0 9.4 %copy-start.2 = (bf16[64,3584]{1,0:T(8,128)(2,1)S(1)}, bf16[64,3584]{1,0:T(8,128)(2,1)}, u32[]{:S(2)}) copy-start(bf16[64,3584]{1,0:T(8,128)(2,1)} %param.9) | copy-start | bytes 1376260
  3.5 5.9 %collective-permute-start = (f32[64,512]{1,0:T(8,128)S(1)}, f32[64,512]{1,0:T(8,128)S(1)}, u32[]{:S(2)}, u32[]{:S(2)}) collective-permute-start(f32[64,512]{1,0:T(8,128)S(1)} %fusion.15), channel_id=1, source_target_pairs={{0,1},{1,0},{2,3},{3,2},{4,5},{5,4},{6,7},{7,6},{8,9},{9,8},{10,11... | collective-permute-start | bytes 393224 | tf_op jit(solution)/shard_map/ppermute | solution.py:34
  4.5 1.4 %collective-permute-start.1 = (f32[64,512]{1,0:T(8,128)S(1)}, f32[64,512]{1,0:T(8,128)S(1)}, u32[]{:S(2)}, u32[]{:S(2)}) collective-permute-start(f32[64,512]{1,0:T(8,128)S(1)} %convolution_bitcast_fusion), channel_id=1, source_target_pairs={{0,1},{1,0},{2,3},{3,2},{4,5},{5,4},{6,7},{7,6},{8,9},{9,8},{10,11... | collective-permute-start | bytes 393224 | tf_op jit(solution)/shard_map/ppermute | solution.py:30
  6.3 14.0 %copy-start.4 = (s32[16]{0:T(128)S(1)}, s32[16]{0:T(128)}, u32[]{:S(2)}) copy-start(s32[16]{0:T(128)} %param.12) | copy-start | bytes 196
  6.4 6.7 %collective-permute-start.2 = (f32[64,512]{1,0:T(8,128)S(1)}, f32[64,512]{1,0:T(8,128)S(1)}, u32[]{:S(2)}, u32[]{:S(2)}) collective-permute-start(f32[64,512]{1,0:T(8,128)S(1)} %fusion.18), channel_id=1, source_target_pairs={{0,2},{1,3},{2,0},{3,1},{4,6},{5,7},{6,4},{7,5},{8,10},{9,11},{10,... | collective-permute-start | bytes 393224 | tf_op jit(solution)/shard_map/ppermute | solution.py:31
  14.3 14.3 %all-to-all-start = ((f32[32,1,1024]{2,1,0:T(1,128)}), f32[32,1,1024]{2,1,0:T(1,128)S(1)}, u32[]{:S(2)}, u32[]{:S(2)}) async-start(f32[32,1,1024]{2,1,0:T(1,128)} %all_to_all.8), calls=%async_computation | async-start | bytes 262144 | tf_op jit(solution)/shard_map/all_to_all | solution.py:44
  31.4 3.2 %collective-permute-start.5 = (f32[4,1024]{1,0:T(4,128)S(1)}, f32[4,1024]{1,0:T(4,128)S(1)}, u32[]{:S(2)}, u32[]{:S(2)}) collective-permute-start(f32[4,1024]{1,0:T(4,128)S(1)} %get-tuple-element.6), channel_id=1, source_target_pairs={{0,3},{1,2},{2,1},{3,0},{4,7},{5,6},{6,5},{7,4},{8,11},{9,10},{10,... | collective-permute-start | bytes 49160 | tf_op jit(solution)/shard_map/ppermute | solution.py:79
  31.6 3.8 %collective-permute-start.4 = (f32[4,1024]{1,0:T(4,128)S(1)}, f32[4,1024]{1,0:T(4,128)S(1)}, u32[]{:S(2)}, u32[]{:S(2)}) collective-permute-start(f32[4,1024]{1,0:T(4,128)S(1)} %get-tuple-element.7), channel_id=1, source_target_pairs={{0,2},{1,3},{2,0},{3,1},{4,6},{5,7},{6,4},{7,5},{8,10},{9,11},{10,... | collective-permute-start | bytes 49160 | tf_op jit(solution)/shard_map/ppermute | solution.py:79
  33.3 2.1 %collective-permute-start.3 = (f32[4,1024]{1,0:T(4,128)S(1)}, f32[4,1024]{1,0:T(4,128)S(1)}, u32[]{:S(2)}, u32[]{:S(2)}) collective-permute-start(f32[4,1024]{1,0:T(4,128)S(1)} %get-tuple-element.5), channel_id=1, source_target_pairs={{0,1},{1,0},{2,3},{3,2},{4,5},{5,4},{6,7},{7,6},{8,9},{9,8},{10,11... | collective-permute-start | bytes 49160 | tf_op jit(solution)/shard_map/ppermute | solution.py:79

commit v2 on v0

v2 whole, which is shorter than its diff:
```python
import functools

import jax
import jax.numpy as jnp
from jax import lax
from jax.experimental import pallas as pl
from jax.experimental.pallas import tpu as pltpu
from jax.sharding import PartitionSpec as P

epsilon = 1e-06
VMEM = pl.BlockSpec(memory_space=pltpu.VMEM)
ANY = pl.BlockSpec(memory_space=pl.ANY)
CHUNKS = 2
SMEM = pl.BlockSpec(memory_space=pltpu.SMEM)


def flip(step):
    return [(i, i ^ step) for i in range(4)]


def put_factor(rows, proj, out_ref, start):
    part = lax.dot_general(
        rows, proj, (((1,), (1,)), ((), ())), preferred_element_type=jnp.float32
    )
    out_ref[:, start : start + rows.shape[0]] = part.T


def in_hbm(arr):
    return pltpu.with_memory_space_constraint(arr, pltpu.HBM)


def out_send_kernel(proj_ref, rows_ref, send_ref, proj_held, rows_held, rows_buf, sems):
    core = lax.rem(lax.axis_index("tp"), 2)
    copies = [
        pltpu.make_async_copy(proj_ref, proj_held, sems.at[0]),
        pltpu.make_async_copy(rows_ref.at[1 - core], rows_buf, sems.at[1]),
        pltpu.make_async_copy(rows_ref.at[core], rows_held, sems.at[2]),
    ]
    for copy in copies:
        copy.start()
    for copy in copies:
        copy.wait()
    put_factor(rows_buf[...], proj_held[...], send_ref, 0)


def out_send(proj, rows):
    rank, depth = proj.shape
    _, tokens, _ = rows.shape
    return pl.pallas_call(
        out_send_kernel,
        out_shape=[
            jax.ShapeDtypeStruct((rank, tokens), jnp.float32),
            jax.ShapeDtypeStruct(proj.shape, proj.dtype),
            jax.ShapeDtypeStruct((tokens, depth), rows.dtype),
        ],
        in_specs=[ANY, ANY],
        out_specs=[VMEM, VMEM, VMEM],
        scratch_shapes=[pltpu.VMEM((tokens, depth), rows.dtype), pltpu.SemaphoreType.DMA((3,))],
        compiler_params=pltpu.CompilerParams(vmem_limit_bytes=8 << 20),
        cost_estimate=pl.CostEstimate(
            flops=4 * rank * depth * tokens, bytes_accessed=4 * depth * tokens, transcendentals=0
        ),
    )(in_hbm(proj), in_hbm(rows))


def out_keep_kernel(proj_ref, rows_ref, out_ref):
    put_factor(rows_ref[...], proj_ref[...], out_ref, 0)


def out_keep(proj, rows):
    rank, depth = proj.shape
    tokens, _ = rows.shape
    return pl.pallas_call(
        out_keep_kernel,
        out_shape=jax.ShapeDtypeStruct((rank, tokens), jnp.float32),
        in_specs=[VMEM, VMEM],
        out_specs=VMEM,
        compiler_params=pltpu.CompilerParams(vmem_limit_bytes=8 << 20),
        cost_estimate=pl.CostEstimate(
            flops=4 * rank * depth * tokens, bytes_accessed=2 * depth * tokens, transcendentals=0
        ),
    )(proj, rows)


def add_kernel(left_ref, right_ref, out_ref):
    out_ref[...] = left_ref[...] + right_ref[...]


def add(left, right):
    return pl.pallas_call(
        add_kernel,
        out_shape=jax.ShapeDtypeStruct(left.shape, left.dtype),
        in_specs=[VMEM, VMEM],
        out_specs=VMEM,
        compiler_params=pltpu.CompilerParams(vmem_limit_bytes=4 << 20),
        cost_estimate=pl.CostEstimate(flops=4 * 10**9, bytes_accessed=16 << 20, transcendentals=0),
    )(left, right)


def in_kernel(proj_ref, rows_ref, after_ref, send_ref, keep_ref):
    core = lax.rem(lax.axis_index("tp"), 2)
    tokens = rows_ref.shape[1]
    for swap, out_ref in ((1, send_ref), (0, keep_ref)):
        prompt = lax.rem(core + swap, 2)
        for start in range(0, tokens, 256):
            put_factor(rows_ref[prompt, start : start + 256, :], proj_ref[...], out_ref, start)


def in_factors(proj, rows, after):
    rank, depth = proj.shape
    tokens = rows.shape[1]
    return pl.pallas_call(
        in_kernel,
        out_shape=[jax.ShapeDtypeStruct((rank, tokens), jnp.float32)] * 2,
        in_specs=[VMEM, VMEM, ANY],
        out_specs=[VMEM, VMEM],
        compiler_params=pltpu.CompilerParams(vmem_limit_bytes=8 << 20),
        cost_estimate=pl.CostEstimate(
            flops=8 * rank * depth * tokens, bytes_accessed=4 * depth * tokens, transcendentals=0
        ),
    )(proj, rows, after)


def outer_kernel(lengths_ref, in_keep_ref, in_got_ref, out_chip_ref, out_got_ref, send_ref, grads_ref):
    rank, tokens = in_keep_ref.shape
    which = lax.rem(lax.axis_index("tp"), 2)
    positions = lax.broadcasted_iota(jnp.int32, (rank, tokens), 1)
    in_chip = in_keep_ref[...] + in_got_ref[...]
    masked = jnp.where(positions < lengths_ref[which], in_chip, 0.0)
    out_full = out_chip_ref[...] + out_got_ref[...]
    grads_ref[...] = lax.dot_general(
        masked,
        out_full,
        (((1,), (1,)), ((), ())),
        precision=lax.Precision.HIGHEST,
        preferred_element_type=jnp.float32,
    )
    half = rank // 2
    even = grads_ref[pl.ds(0, half, stride=2), :]
    odd = grads_ref[pl.ds(1, half, stride=2), :]
    packed = jnp.concatenate([even, odd], axis=1)
    for target in range(send_ref.shape[0]):
        share = target % 4
        send_ref[target] = packed[share * 8 : share * 8 + 8, :]


def outer(lengths, in_keep, in_got, out_chip, out_got, targets):
    rank, tokens = in_keep.shape
    return pl.pallas_call(
        outer_kernel,
        out_shape=jax.ShapeDtypeStruct((targets, rank // 8, 2 * rank), jnp.float32),
        in_specs=[SMEM, VMEM, VMEM, VMEM, VMEM],
        out_specs=VMEM,
        scratch_shapes=[pltpu.VMEM((rank, rank), jnp.float32)],
        compiler_params=pltpu.CompilerParams(vmem_limit_bytes=8 << 20),
        cost_estimate=pl.CostEstimate(
            flops=12 * rank * rank * tokens, bytes_accessed=4 * rank * tokens, transcendentals=0
        ),
    )(lengths, in_keep, in_got, out_chip, out_got)


def norm_kernel(slab_ref, out_ref, held_ref, sems):
    rows, cols = slab_ref.shape
    step = rows // CHUNKS
    copies = []
    for at in range(CHUNKS):
        span = pl.ds(at * step, step)
        copy = pltpu.make_async_copy(slab_ref.at[span, :], held_ref.at[span, :], sems.at[at])
        copy.start()
        copies.append(copy)
    for chunk, copy in enumerate(copies):
        copy.wait()
        for start in range(chunk * step, (chunk + 1) * step, 128):
            total = jnp.zeros((128, 128), jnp.float32)
            for at in range(0, cols, 128):
                wide = held_ref[start : start + 128, at : at + 128].astype(jnp.float32)
                total = total + wide * wide
            out_ref[:, start : start + 128] = jnp.sum(total.T, axis=0, keepdims=True)


def norms(slab):
    rows, cols = slab.shape
    return pl.pallas_call(
        norm_kernel,
        out_shape=[
            jax.ShapeDtypeStruct((1, rows), jnp.float32),
            jax.ShapeDtypeStruct((rows, cols), slab.dtype),
        ],
        in_specs=[ANY],
        out_specs=[VMEM, VMEM],
        scratch_shapes=[pltpu.SemaphoreType.DMA((CHUNKS,))],
        compiler_params=pltpu.CompilerParams(vmem_limit_bytes=8 << 20),
        cost_estimate=pl.CostEstimate(
            flops=2 * rows * cols, bytes_accessed=2 * rows * cols, transcendentals=0
        ),
    )(in_hbm(slab))


def dots_kernel(pairs_mine, perm_ref, partials_ref, slab_ref, norm_ref, *refs):
    *message_refs, query_ref = refs
    k = lax.axis_index("tp")
    pair_count = query_ref.shape[0]

    def whole(example):
        row = (example // 2) * 4 + lax.rem(example, 2)
        return partials_ref[row] + partials_ref[row + 2]

    for at in range(pair_count):
        pair = (k ^ (at // pairs_mine)) * pairs_mine + at % pairs_mine
        query_ref[at] = whole(perm_ref[2 * pair + 1]) - whole(perm_ref[2 * pair])
    depth = query_ref.shape[1]
    blocks = [query_ref[:, r, :] for r in range(depth)]
    queries = jnp.concatenate(blocks, axis=1)
    query_sq = jnp.sum(queries * queries, axis=1, keepdims=True)
    dots = lax.dot_general(
        queries.astype(jnp.bfloat16),
        slab_ref[...],
        (((1,), (1,)), ((), ())),
        preferred_element_type=jnp.float32,
    )
    rows = slab_ref.shape[0]
    for step, message_ref in enumerate(message_refs):
        mine = slice(step * pairs_mine, (step + 1) * pairs_mine)
        message_ref[0:pairs_mine, 0:rows] = dots[mine]
        message_ref[pairs_mine : pairs_mine + 1, 0:rows] = norm_ref[...]
        message_ref[0:pairs_mine, rows : rows + 128] = jnp.broadcast_to(query_sq[mine], (pairs_mine, 128))
        message_ref[pairs_mine : pairs_mine + 1, rows : rows + 128] = jnp.zeros((1, 128), jnp.float32)


def dots(pair_perm, partials, slab, bank_part, tp_count):
    pair_count = pair_perm.shape[0] // 2
    pairs_mine = pair_count // tp_count
    rows, cols = slab.shape
    message = jax.ShapeDtypeStruct((pairs_mine + 1, rows + 128), jnp.float32)
    return pl.pallas_call(
        functools.partial(dots_kernel, pairs_mine),
        out_shape=[message] * tp_count,
        in_specs=[SMEM, VMEM, VMEM, VMEM],
        out_specs=[VMEM] * tp_count,
        scratch_shapes=[pltpu.VMEM((pair_count, 8, 128), jnp.float32)],
        compiler_params=pltpu.CompilerParams(vmem_limit_bytes=8 << 20),
        cost_estimate=pl.CostEstimate(
            flops=2 * pair_count * rows * cols, bytes_accessed=2 * rows * cols, transcendentals=0
        ),
    )(pair_perm, partials, slab, bank_part)


def scores_kernel(scale, own_ref, *refs):
    *got_refs, out_ref = refs
    total = own_ref[...]
    for got_ref in got_refs:
        total = total + got_ref[...]
    pairs, rows = out_ref.shape
    bank_scale = lax.rsqrt(total[pairs : pairs + 1, 0:rows] + epsilon)
    query_scale = lax.rsqrt(total[0:pairs, rows : rows + 1] + epsilon)
    out_ref[...] = total[0:pairs, 0:rows] * scale * query_scale * bank_scale


def scores(messages, scale):
    pairs = messages[0].shape[0] - 1
    rows = messages[0].shape[1] - 128
    return pl.pallas_call(
        functools.partial(scores_kernel, scale),
        out_shape=jax.ShapeDtypeStruct((pairs, rows), jnp.float32),
        in_specs=[VMEM] * len(messages),
        out_specs=VMEM,
        compiler_params=pltpu.CompilerParams(vmem_limit_bytes=8 << 20),
    )(*messages)


def per_device(hidden, out_grad, proj_in, proj_out, lengths, pair_perm, bank_slab):
    rank = proj_in.shape[0]
    tp_count = lax.axis_size("tp")
    bank_count = lax.axis_size("bank")
    out_away, proj_held, rows_held = out_send(proj_out, out_grad)
    out_got = lax.ppermute(out_away, "tp", flip(1))
    out_chip = add(out_keep(proj_held, rows_held), out_got)
    out_other = lax.ppermute(out_chip, "tp", flip(2))
    in_send, in_keep = in_factors(proj_in, hidden, out_chip)
    in_got = lax.ppermute(in_send, "tp", flip(1))
    outgoing = outer(lengths, in_keep, in_got, out_chip, out_other, bank_count * tp_count)
    partials = lax.all_to_all(outgoing, ("bank", "tp"), 0, 0, tiled=True)
    bank_part, held = norms(bank_slab)
    messages = dots(pair_perm, partials, held, bank_part, tp_count)
    got = [messages[0]] + [lax.ppermute(messages[step], "tp", flip(step)) for step in range(1, 4)]
    return scores(got, float(rank))


def solution(mesh):
    return jax.shard_map(
        per_device,
        mesh=mesh,
        in_specs=(
            P("bank", None, "tp"),
            P("bank", None, "tp"),
            P(None, "tp"),
            P(None, "tp"),
            P("bank"),
            P(),
            P("bank", "tp"),
        ),
        out_specs=P("tp", "bank"),
        check_vma=False,
    )
```

time: 107 us -> 32.4 us (0.30)
  blocking collectives: 41.4 us -> 0 us
  waiting for transfers between devices: 32.5 us -> 10.6 us
  between operations: 14.1 us -> 0.08 us
  matrix products: 11.7 us -> 0 us
  starting transfers between devices: 0.01 us -> 11.5 us
  Pallas kernels: 0 us -> 10 us
  local copies, waits for them, and re-layouts: 4.14 us -> 0.03 us
  other arithmetic: 2.91 us -> 0.01 us
    psum x1 -> x0, waiting for transfers between devices: 32.5 us -> none  [per_device(): in_all, out_all = lax.psum((in_part, out_part), 'tp')]
    all_gather x1 -> x0, blocking collectives: 30.6 us -> none  [per_device(): all_grads = lax.all_gather(grads, 'bank', axis=0, tiled=True)]
    dot_general x5 -> x0, matrix products: 11.7 us -> none  [the longest x1 6.14 us: per_device(): jnp.einsum('rf,tf->rt', proj_in, tok_rows, preferred_element_type=jnp.flo...]
    unnamed x1 -> x0, blocking collectives: 10.9 us -> none
    pallas_call x0 -> x8, Pallas kernels: none -> 10 us  [the longest x1 2.11 us: out_send(): pl.pallas_call(out_send_kernel, out_shape=[jax.ShapeDtypeStruct((rank, to...]
    all_to_all x0 -> x1, waiting for transfers between devices: none -> 6.39 us  [per_device(): partials = lax.all_to_all(outgoing, ('bank', 'tp'), 0, 0, tiled=True)]
    all_to_all x0 -> x1, starting transfers between devices: none -> 6.09 us  [per_device(): partials = lax.all_to_all(outgoing, ('bank', 'tp'), 0, 0, tiled=True)]
    ppermute x0 -> x6, starting transfers between devices: none -> 5.4 us  [the longest x1 2.91 us: per_device(): out_other = lax.ppermute(out_chip, 'tp', flip(2))]
  transfers between devices with their start and end apart: 1 -> 7, of which waited for: 1 -> 4; matrix products, arithmetic and copies ran while one was open for 3% -> 0% of each run, Pallas kernels for 0% -> 14%
where the time goes in v2:
time: 32.4 us; the launch traced here: 32.2 us
  starting transfers between devices  11.5 us (35%)
  waiting for transfers between devices  10.6 us (33%)
  Pallas kernels  10 us (31%)
    all_to_all x1, waiting for transfers between devices, per_device(): partials = lax.all_to_all(outgoing, ('bank', 'tp'), 0, 0, tiled=True)  6.39 us
    all_to_all x1, starting transfers between devices, per_device(): partials = lax.all_to_all(outgoing, ('bank', 'tp'), 0, 0, tiled=True)  6.09 us
    ppermute x1, starting transfers between devices, per_device(): out_other = lax.ppermute(out_chip, 'tp', flip(2))  2.91 us
    ppermute x3, waiting for transfers between devices, per_device(): lax.ppermute(messages[step], 'tp', flip(step))  2.12 us
    pallas_call x1, Pallas kernels, out_send(): pl.pallas_call(out_send_kernel, out_shape=[jax.ShapeDtypeStruct((rank, to...  2.11 us
    pallas_call x1, Pallas kernels, in_factors(): pl.pallas_call(in_kernel, out_shape=[jax.ShapeDtypeStruct((rank, tokens),...  2.1 us
    ppermute x3, starting transfers between devices, per_device(): lax.ppermute(messages[step], 'tp', flip(step))  1.89 us
    pallas_call x1, Pallas kernels, norms(): pl.pallas_call(norm_kernel, out_shape=[jax.ShapeDtypeStruct((1, rows), jn...  1.84 us
  transfers between devices with their start and end apart: 7, of which 4 were waited for; matrix products, arithmetic and copies ran while one was open for 0% of the time, Pallas kernels for 14%

profile of v2, /device:TPU:0, one launch (start us, length us, event | category | flops | bytes accessed | tf_op | source)
XLA Modules:
  0.0 32.2 jit_solution(14961441072745673403)
XLA Ops:
  0.0 2.1 %shard_map.73 = (f32[64,512]{1,0:T(8,128)S(1)}, bf16[64,1024]{1,0:T(8,128)(2,1)S(1)}, bf16[512,1024]{1,0:T(8,128)(2,1)S(1)}) custom-call(bf16[64,1024]{1,0:T(8,128)(2,1)} %proj_ref.2, bf16[2,512,1024]{2,1,0:T(8,128)(2,1)} %rows_ref.2), custom_call_target="tpu_custom_call" | custom-call | flops 134217728 | bytes 2097152 | tf_op jit(solution)/shard_map/pallas_call | solution.py:49
  2.1 0.5 %collective-permute-start = (f32[64,512]{1,0:T(8,128)S(1)}, f32[64,512]{1,0:T(8,128)S(1)}, u32[]{:S(2)}, u32[]{:S(2)}) collective-permute-start(f32[64,512]{1,0:T(8,128)S(1)} %get-tuple-element.18), channel_id=1, source_target_pairs={{0,1},{1,0},{2,3},{3,2},{4,5},{5,4},{6,7},{7,6},{8,9},{9,8},{10,11... | collective-permute-start | bytes 393224 | tf_op jit(solution)/shard_map/ppermute | solution.py:276
  2.6 0.0 slice-start
  2.6 0.5 %shard_map.74.left_ref = f32[64,512]{1,0:T(8,128)S(1)} custom-call(bf16[64,1024]{1,0:T(8,128)(2,1)S(1)} %get-tuple-element.16.proj_ref, bf16[512,1024]{1,0:T(8,128)(2,1)S(1)} %get-tuple-element.17.rows_ref), custom_call_target="tpu_custom_call" | custom-call | flops 134217728 | bytes 1048576 | tf_op jit(solution)/shard_map/pallas_call | solution.py:73
  3.1 0.0 slice-start.1
  3.1 0.0 copy-start
  3.1 0.5 %collective-permute-done.right_ref = f32[64,512]{1,0:T(8,128)S(1)} collective-permute-done((f32[64,512]{1,0:T(8,128)S(1)}, f32[64,512]{1,0:T(8,128)S(1)}, u32[]{:S(2)}, u32[]{:S(2)}) %collective-permute-start) | collective-permute-done | bytes 131104 | tf_op jit(solution)/shard_map/ppermute | solution.py:276
  3.6 0.0 copy-start.2
  3.7 2.9 %collective-permute-start.2 = (f32[64,512]{1,0:T(8,128)S(1)}, f32[64,512]{1,0:T(8,128)S(1)}, u32[]{:S(2)}, u32[]{:S(2)}) collective-permute-start(f32[64,512]{1,0:T(8,128)S(1)} %shard_map.75.after_ref.out_chip_ref), channel_id=1, source_target_pairs={{0,2},{1,3},{2,0},{3,1},{4,6},{5,7},{6,4},{7,5},{8,10},{9,11},{10,... | collective-permute-start | bytes 393224 | tf_op jit(solution)/shard_map/ppermute | solution.py:278
  6.6 0.0 slice-done
  6.6 0.0 slice-done.1
  6.6 0.0 copy-done
  6.6 2.1 %shard_map.76 = (f32[64,512]{1,0:T(8,128)S(1)}, f32[64,512]{1,0:T(8,128)S(1)}) custom-call(bf16[64,3584]{1,0:T(8,128)(2,1)S(1)} %copy-done, bf16[2,512,3584]{2,1,0:T(8,128)(2,1)S(1)} %bitcast.1, f32[64,512]{1,0:T(8,128)S(1)} %shard_map.75.after_ref.out_chip_ref), custom_call_target="tpu_custom_call" | custom-call | flops 939524096 | bytes 7340032 | tf_op jit(solution)/shard_map/pallas_call | solution.py:112
  8.7 0.0 copy-start.1
  8.7 0.1 collective-permute-start.1
  8.8 1.6 %collective-permute-done.2.out_got_ref = f32[64,512]{1,0:T(8,128)S(1)} collective-permute-done((f32[64,512]{1,0:T(8,128)S(1)}, f32[64,512]{1,0:T(8,128)S(1)}, u32[]{:S(2)}, u32[]{:S(2)}) %collective-permute-start.2) | collective-permute-done | bytes 131104 | tf_op jit(solution)/shard_map/ppermute | solution.py:278
  10.4 0.0 collective-permute-done.1.in_got_ref
  10.4 0.0 copy-done.2
  10.4 1.6 %shard_map.77 = f32[32,8,128]{2,1,0:T(8,128)} custom-call(s32[2]{0:T(128)S(1)} %copy-done.2, f32[64,512]{1,0:T(8,128)S(1)} %get-tuple-element.19.in_keep_ref, f32[64,512]{1,0:T(8,128)S(1)} %collective-permute-done.1.in_got_ref, f32[64,512]{1,0:T(8,128)S(1)} %shard_map.75.after_ref.out_chip_ref, f32[64,512]{1,0:T(8,128)S(1)} %collective-permute-done.2.out_got_ref), custom_call_target="tpu_custom_call" | custom-call | flops 25165824 | bytes 131072 | tf_op jit(solution)/shard_map/pallas_call | solution.py:149
  12.0 6.1 %all-to-all-start = ((f32[32,8,128]{2,1,0:T(8,128)}), f32[32,8,128]{2,1,0:T(8,128)S(1)}, u32[]{:S(2)}, u32[]{:S(2)}) async-start(f32[32,8,128]{2,1,0:T(8,128)} %shard_map.77), calls=%async_computation | async-start | bytes 262144 | tf_op jit(solution)/shard_map/all_to_all | solution.py:282
  18.1 1.8 %shard_map.78 = (f32[1,1024]{1,0:T(1,128)S(1)}, bf16[1024,1024]{1,0:T(8,128)(2,1)S(1)}) custom-call(bf16[1024,1024]{1,0:T(8,128)(2,1)} %slab_ref.1), custom_call_target="tpu_custom_call" | custom-call | flops 2097152 | bytes 2097152 | tf_op jit(solution)/shard_map/pallas_call | solution.py:183
  19.9 6.4 %all-to-all-done.partials_ref = f32[32,8,128]{2,1,0:T(8,128)S(1)} async-done(((f32[32,8,128]{2,1,0:T(8,128)}), f32[32,8,128]{2,1,0:T(8,128)S(1)}, u32[]{:S(2)}, u32[]{:S(2)}) %all-to-all-start) | async-done | bytes 131104 | tf_op jit(solution)/shard_map/all_to_all | solution.py:282
  26.3 0.0 copy-done.1
  26.3 1.2 %shard_map.79 = (f32[3,1152]{1,0:T(4,128)S(1)}, f32[3,1152]{1,0:T(4,128)S(1)}, f32[3,1152]{1,0:T(4,128)S(1)}, f32[3,1152]{1,0:T(4,128)S(1)}) custom-call(s32[16]{0:T(128)S(1)} %copy-done.1, f32[32,8,128]{2,1,0:T(8,128)S(1)} %all-to-all-done.partials_ref, bf16[1024,1024]{1,0:T(8,128)(2,1)S(1)} %get-tuple-element.21.slab_ref, ...), custom_call_target="tpu_custom_call" | custom-call | flops 16777216 | bytes 2097152 | tf_op jit(solution)/shard_map/pallas_call | solution.py:235
  27.5 0.2 collective-permute-start.3
  27.8 0.4 %collective-permute-start.4 = (f32[3,1152]{1,0:T(4,128)S(1)}, f32[3,1152]{1,0:T(4,128)S(1)}, u32[]{:S(2)}, u32[]{:S(2)}) collective-permute-start(f32[3,1152]{1,0:T(4,128)S(1)} %get-tuple-element.25), channel_id=1, source_target_pairs={{0,2},{1,3},{2,0},{3,1},{4,6},{5,7},{6,4},{7,5},{8,10},{9,11},{10,... | collective-permute-start | bytes 41480 | tf_op jit(solution)/shard_map/ppermute | solution.py:285
  28.1 1.3 %collective-permute-start.5 = (f32[3,1152]{1,0:T(4,128)S(1)}, f32[3,1152]{1,0:T(4,128)S(1)}, u32[]{:S(2)}, u32[]{:S(2)}) collective-permute-start(f32[3,1152]{1,0:T(4,128)S(1)} %get-tuple-element.26), channel_id=1, source_target_pairs={{0,3},{1,2},{2,1},{3,0},{4,7},{5,6},{6,5},{7,4},{8,11},{9,10},{10,... | collective-permute-start | bytes 41480 | tf_op jit(solution)/shard_map/ppermute | solution.py:285
  29.4 0.0 collective-permute-done.3.refs_0_
  29.4 2.1 %collective-permute-done.4.refs_1_ = f32[3,1152]{1,0:T(4,128)S(1)} collective-permute-done((f32[3,1152]{1,0:T(4,128)S(1)}, f32[3,1152]{1,0:T(4,128)S(1)}, u32[]{:S(2)}, u32[]{:S(2)}) %collective-permute-start.4) | collective-permute-done | bytes 13856 | tf_op jit(solution)/shard_map/ppermute | solution.py:285
  31.5 0.0 collective-permute-done.5.refs_2_
  31.5 0.7 %shard_map.80 = f32[2,1024]{1,0:T(2,128)} custom-call(f32[3,1152]{1,0:T(4,128)S(1)} %get-tuple-element.23.own_ref, f32[3,1152]{1,0:T(4,128)S(1)} %collective-permute-done.3.refs_0_, f32[3,1152]{1,0:T(4,128)S(1)} %collective-permute-done.4.refs_1_, f32[3,1152]{1,0:T(4,128)S(1)} %collective-permute-done.5.refs_2_), custom_call_target="tpu_custom_call" | custom-call | tf_op jit(solution)/shard_map/pallas_call | solution.py:262
  (2 shorter events, 0.0 us)
Async XLA Ops:
  2.1 1.5 %collective-permute-start = (f32[64,512]{1,0:T(8,128)S(1)}, f32[64,512]{1,0:T(8,128)S(1)}, u32[]{:S(2)}, u32[]{:S(2)}) collective-permute-start(f32[64,512]{1,0:T(8,128)S(1)} %get-tuple-element.18), channel_id=1, source_target_pairs={{0,1},{1,0},{2,3},{3,2},{4,5},{5,4},{6,7},{7,6},{8,9},{9,8},{10,11... | collective-permute-start | bytes 393224 | tf_op jit(solution)/shard_map/ppermute | solution.py:276
  2.6 3.9 %slice-start = ((s8[7340032]{0:T(1024)(128)(4,1)}), s8[3145728]{0:T(1024)(128)(4,1)S(1)}, s32[]{:S(2)}) async-start(s8[7340032]{0:T(1024)(128)(4,1)} %bitcast), calls=%async_computation.1 | async-start | bytes 6291456
  3.1 3.5 %slice-start.1 = ((s8[7340032]{0:T(1024)(128)(4,1)}), s8[4194304]{0:T(1024)(128)(4,1)S(1)}, s32[]{:S(2)}) async-start(s8[7340032]{0:T(1024)(128)(4,1)} %bitcast), calls=%async_computation.2 | async-start | bytes 8388608
  3.1 3.5 %copy-start = (bf16[64,3584]{1,0:T(8,128)(2,1)S(1)}, bf16[64,3584]{1,0:T(8,128)(2,1)}, u32[]{:S(2)}) copy-start(bf16[64,3584]{1,0:T(8,128)(2,1)} %proj_ref.3) | copy-start | bytes 1376260
  3.6 6.7 %copy-start.2 = (s32[2]{0:T(128)S(1)}, s32[2]{0:T(128)}, u32[]{:S(2)}) copy-start(s32[2]{0:T(128)} %lengths_ref.1) | copy-start | bytes 28
  3.7 6.7 %collective-permute-start.2 = (f32[64,512]{1,0:T(8,128)S(1)}, f32[64,512]{1,0:T(8,128)S(1)}, u32[]{:S(2)}, u32[]{:S(2)}) collective-permute-start(f32[64,512]{1,0:T(8,128)S(1)} %shard_map.75.after_ref.out_chip_ref), channel_id=1, source_target_pairs={{0,2},{1,3},{2,0},{3,1},{4,6},{5,7},{6,4},{7,5},{8,10},{9,11},{10,... | collective-permute-start | bytes 393224 | tf_op jit(solution)/shard_map/ppermute | solution.py:278
  8.7 17.6 %copy-start.1 = (s32[16]{0:T(128)S(1)}, s32[16]{0:T(128)}, u32[]{:S(2)}) copy-start(s32[16]{0:T(128)} %perm_ref.1) | copy-start | bytes 196
  8.7 1.7 %collective-permute-start.1 = (f32[64,512]{1,0:T(8,128)S(1)}, f32[64,512]{1,0:T(8,128)S(1)}, u32[]{:S(2)}, u32[]{:S(2)}) collective-permute-start(f32[64,512]{1,0:T(8,128)S(1)} %get-tuple-element.20), channel_id=1, source_target_pairs={{0,1},{1,0},{2,3},{3,2},{4,5},{5,4},{6,7},{7,6},{8,9},{9,8},{10,11... | collective-permute-start | bytes 393224 | tf_op jit(solution)/shard_map/ppermute | solution.py:280
  12.0 14.3 %all-to-all-start = ((f32[32,8,128]{2,1,0:T(8,128)}), f32[32,8,128]{2,1,0:T(8,128)S(1)}, u32[]{:S(2)}, u32[]{:S(2)}) async-start(f32[32,8,128]{2,1,0:T(8,128)} %shard_map.77), calls=%async_computation | async-start | bytes 262144 | tf_op jit(solution)/shard_map/all_to_all | solution.py:282
  27.5 1.9 %collective-permute-start.3 = (f32[3,1152]{1,0:T(4,128)S(1)}, f32[3,1152]{1,0:T(4,128)S(1)}, u32[]{:S(2)}, u32[]{:S(2)}) collective-permute-start(f32[3,1152]{1,0:T(4,128)S(1)} %get-tuple-element.24), channel_id=1, source_target_pairs={{0,1},{1,0},{2,3},{3,2},{4,5},{5,4},{6,7},{7,6},{8,9},{9,8},{10,11... | collective-permute-start | bytes 41480 | tf_op jit(solution)/shard_map/ppermute | solution.py:285
  27.8 3.8 %collective-permute-start.4 = (f32[3,1152]{1,0:T(4,128)S(1)}, f32[3,1152]{1,0:T(4,128)S(1)}, u32[]{:S(2)}, u32[]{:S(2)}) collective-permute-start(f32[3,1152]{1,0:T(4,128)S(1)} %get-tuple-element.25), channel_id=1, source_target_pairs={{0,2},{1,3},{2,0},{3,1},{4,6},{5,7},{6,4},{7,5},{8,10},{9,11},{10,... | collective-permute-start | bytes 41480 | tf_op jit(solution)/shard_map/ppermute | solution.py:285
  28.1 3.4 %collective-permute-start.5 = (f32[3,1152]{1,0:T(4,128)S(1)}, f32[3,1152]{1,0:T(4,128)S(1)}, u32[]{:S(2)}, u32[]{:S(2)}) collective-permute-start(f32[3,1152]{1,0:T(4,128)S(1)} %get-tuple-element.26), channel_id=1, source_target_pairs={{0,3},{1,2},{2,1},{3,0},{4,7},{5,6},{6,5},{7,4},{8,11},{9,10},{10,... | collective-permute-start | bytes 41480 | tf_op jit(solution)/shard_map/ppermute | solution.py:285

commit v3 on v2

--- a/solution.py
+++ b/solution.py
@@ -10,8 +10,6 @@
 epsilon = 1e-06
 VMEM = pl.BlockSpec(memory_space=pltpu.VMEM)
 ANY = pl.BlockSpec(memory_space=pl.ANY)
-CHUNKS = 2
-SMEM = pl.BlockSpec(memory_space=pltpu.SMEM)
 
 
 def flip(step):
@@ -32,15 +30,16 @@
 def out_send_kernel(proj_ref, rows_ref, send_ref, proj_held, rows_held, rows_buf, sems):
     core = lax.rem(lax.axis_index("tp"), 2)
     copies = [
-        pltpu.make_async_copy(proj_ref, proj_held, sems.at[0]),
-        pltpu.make_async_copy(rows_ref.at[1 - core], rows_buf, sems.at[1]),
+        pltpu.make_async_copy(rows_ref.at[1 - core], rows_buf, sems.at[0]),
+        pltpu.make_async_copy(proj_ref, proj_held, sems.at[1]),
         pltpu.make_async_copy(rows_ref.at[core], rows_held, sems.at[2]),
     ]
     for copy in copies:
         copy.start()
-    for copy in copies:
-        copy.wait()
+    copies[0].wait()
+    copies[1].wait()
     put_factor(rows_buf[...], proj_held[...], send_ref, 0)
+    copies[2].wait()
 
 
 def out_send(proj, rows):
@@ -82,19 +81,20 @@
     )(proj, rows)
 
 
-def add_kernel(left_ref, right_ref, out_ref):
+def add_kernel(left_ref, right_ref, *refs):
+    out_ref = refs[-1]
     out_ref[...] = left_ref[...] + right_ref[...]
 
 
-def add(left, right):
+def add(left, right, *after):
     return pl.pallas_call(
         add_kernel,
         out_shape=jax.ShapeDtypeStruct(left.shape, left.dtype),
-        in_specs=[VMEM, VMEM],
+        in_specs=[VMEM, VMEM] + [ANY] * len(after),
         out_specs=VMEM,
         compiler_params=pltpu.CompilerParams(vmem_limit_bytes=4 << 20),
         cost_estimate=pl.CostEstimate(flops=4 * 10**9, bytes_accessed=16 << 20, transcendentals=0),
-    )(left, right)
+    )(left, right, *after)
 
 
 def in_kernel(proj_ref, rows_ref, after_ref, send_ref, keep_ref):
@@ -121,12 +121,9 @@
     )(proj, rows, after)
 
 
-def outer_kernel(lengths_ref, in_keep_ref, in_got_ref, out_chip_ref, out_got_ref, send_ref, grads_ref):
-    rank, tokens = in_keep_ref.shape
-    which = lax.rem(lax.axis_index("tp"), 2)
-    positions = lax.broadcasted_iota(jnp.int32, (rank, tokens), 1)
-    in_chip = in_keep_ref[...] + in_got_ref[...]
-    masked = jnp.where(positions < lengths_ref[which], in_chip, 0.0)
+def outer_kernel(live_ref, in_keep_ref, in_got_ref, out_chip_ref, out_got_ref, after_ref, send_ref, grads_ref):
+    rank = in_keep_ref.shape[0]
+    masked = jnp.where(live_ref[...] > 0.0, in_keep_ref[...] + in_got_ref[...], 0.0)
     out_full = out_chip_ref[...] + out_got_ref[...]
     grads_ref[...] = lax.dot_general(
         masked,
@@ -144,73 +141,58 @@
         send_ref[target] = packed[share * 8 : share * 8 + 8, :]
 
 
-def outer(lengths, in_keep, in_got, out_chip, out_got, targets):
+def outer(live, in_keep, in_got, out_chip, out_got, after, targets):
     rank, tokens = in_keep.shape
     return pl.pallas_call(
         outer_kernel,
         out_shape=jax.ShapeDtypeStruct((targets, rank // 8, 2 * rank), jnp.float32),
-        in_specs=[SMEM, VMEM, VMEM, VMEM, VMEM],
+        in_specs=[VMEM, VMEM, VMEM, VMEM, VMEM, ANY],
         out_specs=VMEM,
         scratch_shapes=[pltpu.VMEM((rank, rank), jnp.float32)],
         compiler_params=pltpu.CompilerParams(vmem_limit_bytes=8 << 20),
         cost_estimate=pl.CostEstimate(
             flops=12 * rank * rank * tokens, bytes_accessed=4 * rank * tokens, transcendentals=0
         ),
-    )(lengths, in_keep, in_got, out_chip, out_got)
-
-
-def norm_kernel(slab_ref, out_ref, held_ref, sems):
+    )(live, in_keep, in_got, out_chip, out_got, after)
+
+
+def norm_kernel(slab_ref, after_ref, out_ref):
     rows, cols = slab_ref.shape
-    step = rows // CHUNKS
-    copies = []
-    for at in range(CHUNKS):
-        span = pl.ds(at * step, step)
-        copy = pltpu.make_async_copy(slab_ref.at[span, :], held_ref.at[span, :], sems.at[at])
-        copy.start()
-        copies.append(copy)
-    for chunk, copy in enumerate(copies):
-        copy.wait()
-        for start in range(chunk * step, (chunk + 1) * step, 128):
-            total = jnp.zeros((128, 128), jnp.float32)
-            for at in range(0, cols, 128):
-                wide = held_ref[start : start + 128, at : at + 128].astype(jnp.float32)
-                total = total + wide * wide
-            out_ref[:, start : start + 128] = jnp.sum(total.T, axis=0, keepdims=True)
-
-
-def norms(slab):
+    for start in range(0, rows, 128):
+        total = jnp.zeros((128, 128), jnp.float32)
+        for at in range(0, cols, 128):
+            wide = slab_ref[start : start + 128, at : at + 128].astype(jnp.float32)
+            total = total + wide * wide
+        out_ref[:, start : start + 128] = jnp.sum(total.T, axis=0, keepdims=True)
+
+
+def norms(slab, after):
     rows, cols = slab.shape
     return pl.pallas_call(
         norm_kernel,
-        out_shape=[
-            jax.ShapeDtypeStruct((1, rows), jnp.float32),
-            jax.ShapeDtypeStruct((rows, cols), slab.dtype),
-        ],
-        in_specs=[ANY],
-        out_specs=[VMEM, VMEM],
-        scratch_shapes=[pltpu.SemaphoreType.DMA((CHUNKS,))],
+        out_shape=jax.ShapeDtypeStruct((1, rows), jnp.float32),
+        in_specs=[VMEM, ANY],
+        out_specs=VMEM,
         compiler_params=pltpu.CompilerParams(vmem_limit_bytes=8 << 20),
         cost_estimate=pl.CostEstimate(
             flops=2 * rows * cols, bytes_accessed=2 * rows * cols, transcendentals=0
         ),
-    )(in_hbm(slab))
-
-
-def dots_kernel(pairs_mine, perm_ref, partials_ref, slab_ref, norm_ref, *refs):
-    *message_refs, query_ref = refs
-    k = lax.axis_index("tp")
-    pair_count = query_ref.shape[0]
-
-    def whole(example):
-        row = (example // 2) * 4 + lax.rem(example, 2)
-        return partials_ref[row] + partials_ref[row + 2]
-
-    for at in range(pair_count):
-        pair = (k ^ (at // pairs_mine)) * pairs_mine + at % pairs_mine
-        query_ref[at] = whole(perm_ref[2 * pair + 1]) - whole(perm_ref[2 * pair])
-    depth = query_ref.shape[1]
-    blocks = [query_ref[:, r, :] for r in range(depth)]
-    queries = jnp.concatenate(blocks, axis=1)
+    )(slab, after)
+
+
+def dots_kernel(signs_ref, partials_ref, slab_ref, norm_ref, *message_refs):
+    pair_count = signs_ref.shape[0]
+    pairs_mine = pair_count // len(message_refs)
+    rows = slab_ref.shape[0]
+    blocks = [partials_ref[:, r, :] for r in range(partials_ref.shape[1])]
+    partials = jnp.concatenate(blocks, axis=1)
+    queries = lax.dot_general(
+        signs_ref[...],
+        partials,
+        (((1,), (0,)), ((), ())),
+        precision=lax.Precision.HIGHEST,
+        preferred_element_type=jnp.float32,
+    )
     query_sq = jnp.sum(queries * queries, axis=1, keepdims=True)
     dots = lax.dot_general(
         queries.astype(jnp.bfloat16),
@@ -218,7 +200,6 @@
         (((1,), (1,)), ((), ())),
         preferred_element_type=jnp.float32,
     )
-    rows = slab_ref.shape[0]
     for step, message_ref in enumerate(message_refs):
         mine = slice(step * pairs_mine, (step + 1) * pairs_mine)
         message_ref[0:pairs_mine, 0:rows] = dots[mine]
@@ -227,22 +208,35 @@
         message_ref[pairs_mine : pairs_mine + 1, rows : rows + 128] = jnp.zeros((1, 128), jnp.float32)
 
 
-def dots(pair_perm, partials, slab, bank_part, tp_count):
+def dots(signs, partials, slab, bank_part, tp_count):
+    pair_count = signs.shape[0]
+    rows, cols = slab.shape
+    message = jax.ShapeDtypeStruct((pair_count // tp_count + 1, rows + 128), jnp.float32)
+    return pl.pallas_call(
+        dots_kernel,
+        out_shape=[message] * tp_count,
+        in_specs=[VMEM, VMEM, VMEM, VMEM],
+        out_specs=[VMEM] * tp_count,
+        compiler_params=pltpu.CompilerParams(vmem_limit_bytes=8 << 20),
+        cost_estimate=pl.CostEstimate(
+            flops=2 * pair_count * rows * cols, bytes_accessed=2 * rows * cols, transcendentals=0
+        ),
+    )(signs, partials, slab, bank_part)
+
+
+def pair_signs(pair_perm, sources, tp_count):
+    slots = jnp.arange(pair_perm.shape[0], dtype=jnp.int32)
     pair_count = pair_perm.shape[0] // 2
     pairs_mine = pair_count // tp_count
-    rows, cols = slab.shape
-    message = jax.ShapeDtypeStruct((pairs_mine + 1, rows + 128), jnp.float32)
-    return pl.pallas_call(
-        functools.partial(dots_kernel, pairs_mine),
-        out_shape=[message] * tp_count,
-        in_specs=[SMEM, VMEM, VMEM, VMEM],
-        out_specs=[VMEM] * tp_count,
-        scratch_shapes=[pltpu.VMEM((pair_count, 8, 128), jnp.float32)],
-        compiler_params=pltpu.CompilerParams(vmem_limit_bytes=8 << 20),
-        cost_estimate=pl.CostEstimate(
-            flops=2 * pair_count * rows * cols, bytes_accessed=2 * rows * cols, transcendentals=0
-        ),
-    )(pair_perm, partials, slab, bank_part)
+    order = jnp.arange(pair_count, dtype=jnp.int32)
+    pair = ((order // pairs_mine) ^ lax.axis_index("tp")) * pairs_mine + order % pairs_mine
+    weights = (slots[None, :] == 2 * pair[:, None] + 1).astype(jnp.float32) - (
+        slots[None, :] == 2 * pair[:, None]
+    ).astype(jnp.float32)
+    source = jnp.arange(sources, dtype=jnp.int32)
+    example = (source // tp_count) * 2 + source % 2
+    hits = (pair_perm[None, :, None] == example[None, None, :]).astype(jnp.float32)
+    return jnp.sum(weights[:, :, None] * hits, axis=1)
 
 
 def scores_kernel(scale, own_ref, *refs):
@@ -268,20 +262,30 @@
     )(*messages)
 
 
+def live_row(lengths, tokens):
+    prompts = jnp.arange(lengths.shape[0], dtype=jnp.int32)
+    positions = jnp.arange(tokens, dtype=jnp.int32)
+    mine = prompts == lax.rem(lax.axis_index("tp"), 2)
+    live = mine[:, None] & (positions[None, :] < lengths[:, None])
+    return jnp.sum(live.astype(jnp.float32), axis=0, keepdims=True)
+
+
 def per_device(hidden, out_grad, proj_in, proj_out, lengths, pair_perm, bank_slab):
     rank = proj_in.shape[0]
     tp_count = lax.axis_size("tp")
     bank_count = lax.axis_size("bank")
+    live = live_row(lengths, hidden.shape[1])
+    signs = pair_signs(pair_perm, bank_count * tp_count, tp_count)
     out_away, proj_held, rows_held = out_send(proj_out, out_grad)
     out_got = lax.ppermute(out_away, "tp", flip(1))
-    out_chip = add(out_keep(proj_held, rows_held), out_got)
+    out_chip = add(out_keep(proj_held, rows_held), out_got, live, signs)
     out_other = lax.ppermute(out_chip, "tp", flip(2))
-    in_send, in_keep = in_factors(proj_in, hidden, out_chip)
-    in_got = lax.ppermute(in_send, "tp", flip(1))
-    outgoing = outer(lengths, in_keep, in_got, out_chip, out_other, bank_count * tp_count)
+    in_away, in_keep = in_factors(proj_in, hidden, out_chip)
+    in_got = lax.ppermute(in_away, "tp", flip(1))
+    bank_part = norms(bank_slab, in_away)
+    outgoing = outer(live, in_keep, in_got, out_chip, out_other, bank_part, bank_count * tp_count)
     partials = lax.all_to_all(outgoing, ("bank", "tp"), 0, 0, tiled=True)
-    bank_part, held = norms(bank_slab)
-    messages = dots(pair_perm, partials, held, bank_part, tp_count)
+    messages = dots(signs, partials, bank_slab, bank_part, tp_count)
     got = [messages[0]] + [lax.ppermute(messages[step], "tp", flip(step)) for step in range(1, 4)]
     return scores(got, float(rank))
 

time: 32.4 us -> 30.4 us (0.938)
  blocking collectives: 0 us -> 14.4 us
  waiting for transfers between devices: 10.6 us -> 3.37 us
  starting transfers between devices: 11.5 us -> 5.38 us
  Pallas kernels: 10 us -> 6.63 us
  other arithmetic: 0.01 us -> 0.35 us
    all_to_all x0 -> x1, blocking collectives: none -> 14.4 us  [per_device(): partials = lax.all_to_all(outgoing, ('bank', 'tp'), 0, 0, tiled=True)]
    all_to_all x1 -> x0, waiting for transfers between devices: 6.39 us -> none  [per_device(): partials = lax.all_to_all(outgoing, ('bank', 'tp'), 0, 0, tiled=True)]
    all_to_all x1 -> x0, starting transfers between devices: 6.09 us -> none  [per_device(): partials = lax.all_to_all(outgoing, ('bank', 'tp'), 0, 0, tiled=True)]
    pallas_call x2, Pallas kernels: 3.06 us -> 1.25 us  [the longest x1 0.77 us: dots(): pl.pallas_call(dots_kernel, out_shape=[message] * tp_count, in_specs=[VME...]
    pallas_call x1, Pallas kernels: 1.57 us -> 0.35 us  [outer(): pl.pallas_call(outer_kernel, out_shape=jax.ShapeDtypeStruct((targets, ran...]
    ppermute x1, waiting for transfers between devices: 1.6 us -> 1.13 us  [per_device(): out_other = lax.ppermute(out_chip, 'tp', flip(2))]
    ppermute x1, waiting for transfers between devices: 0.5 us -> 0.13 us  [per_device(): out_got = lax.ppermute(out_away, 'tp', flip(1))]
    pallas_call x1, Pallas kernels: 2.11 us -> 1.76 us  [out_send(): pl.pallas_call(out_send_kernel, out_shape=[jax.ShapeDtypeStruct((rank, to...]
  transfers between devices with their start and end apart: 7 -> 6, of which waited for: 4 -> 3; matrix products, arithmetic and copies ran while one was open for 0% -> 1% of each run, Pallas kernels for 14% -> 10%
where the time goes in v3:
time: 30.4 us; the launch traced here: 30.3 us
  blocking collectives  14.4 us (47%)
  Pallas kernels  6.63 us (22%)
  starting transfers between devices  5.38 us (18%)
  waiting for transfers between devices  3.37 us (11%)
  other arithmetic  0.35 us (1%)
    all_to_all x1, blocking collectives, per_device(): partials = lax.all_to_all(outgoing, ('bank', 'tp'), 0, 0, tiled=True)  14.4 us
    ppermute x1, starting transfers between devices, per_device(): out_other = lax.ppermute(out_chip, 'tp', flip(2))  2.91 us
    ppermute x3, waiting for transfers between devices, per_device(): lax.ppermute(messages[step], 'tp', flip(step))  2.12 us
    pallas_call x1, Pallas kernels, in_factors(): pl.pallas_call(in_kernel, out_shape=[jax.ShapeDtypeStruct((rank, tokens),...  2.11 us
    ppermute x3, starting transfers between devices, per_device(): lax.ppermute(messages[step], 'tp', flip(step))  1.88 us
    pallas_call x1, Pallas kernels, out_send(): pl.pallas_call(out_send_kernel, out_shape=[jax.ShapeDtypeStruct((rank, to...  1.76 us
    ppermute x1, waiting for transfers between devices, per_device(): out_other = lax.ppermute(out_chip, 'tp', flip(2))  1.13 us
    pallas_call x1, Pallas kernels, dots(): pl.pallas_call(dots_kernel, out_shape=[message] * tp_count, in_specs=[VME...  0.77 us
  transfers between devices with their start and end apart: 6, of which 3 were waited for; matrix products, arithmetic and copies ran while one was open for 1% of the time, Pallas kernels for 10%

profile of v3, /device:TPU:0, one launch (start us, length us, event | category | flops | bytes accessed | tf_op | source)
XLA Modules:
  0.0 30.3 jit_solution(9969741999782899842)
XLA Ops:
  0.0 0.0 copy-start.2
  0.0 0.0 copy-start.3
  0.0 1.8 %shard_map.73 = (f32[64,512]{1,0:T(8,128)S(1)}, bf16[64,1024]{1,0:T(8,128)(2,1)S(1)}, bf16[512,1024]{1,0:T(8,128)(2,1)S(1)}) custom-call(bf16[64,1024]{1,0:T(8,128)(2,1)} %proj_ref.2, bf16[2,512,1024]{2,1,0:T(8,128)(2,1)} %rows_ref.2), custom_call_target="tpu_custom_call" | custom-call | flops 134217728 | bytes 2097152 | tf_op jit(solution)/shard_map/pallas_call | solution.py:48
  1.8 0.5 %collective-permute-start = (f32[64,512]{1,0:T(8,128)S(1)}, f32[64,512]{1,0:T(8,128)S(1)}, u32[]{:S(2)}, u32[]{:S(2)}) collective-permute-start(f32[64,512]{1,0:T(8,128)S(1)} %get-tuple-element.16), channel_id=1, source_target_pairs={{0,1},{1,0},{2,3},{3,2},{4,5},{5,4},{6,7},{7,6},{8,9},{9,8},{10,11... | collective-permute-start | bytes 393224 | tf_op jit(solution)/shard_map/ppermute | solution.py:280
  2.3 0.1 convert_subtract_fusion
  2.4 0.0 copy-done.2
  2.4 0.1 compare_convert_fusion
  2.4 0.1 multiply_reduce_fusion.refs_1_.signs_ref
  2.6 0.0 slice-start
  2.6 0.5 %shard_map.74.left_ref = f32[64,512]{1,0:T(8,128)S(1)} custom-call(bf16[64,1024]{1,0:T(8,128)(2,1)S(1)} %get-tuple-element.14.proj_ref, bf16[512,1024]{1,0:T(8,128)(2,1)S(1)} %get-tuple-element.15.rows_ref), custom_call_target="tpu_custom_call" | custom-call | flops 134217728 | bytes 1048576 | tf_op jit(solution)/shard_map/pallas_call | solution.py:72
  3.0 0.0 copy-done.3
  3.1 0.1 fusion
  3.1 0.1 collective-permute-done.right_ref
  3.3 0.0 slice-start.1
  3.3 0.0 copy-start.1
  3.3 0.0 copy-start
  3.3 2.9 %collective-permute-start.2 = (f32[64,512]{1,0:T(8,128)S(1)}, f32[64,512]{1,0:T(8,128)S(1)}, u32[]{:S(2)}, u32[]{:S(2)}) collective-permute-start(f32[64,512]{1,0:T(8,128)S(1)} %shard_map.75.after_ref.out_chip_ref), channel_id=1, source_target_pairs={{0,2},{1,3},{2,0},{3,1},{4,6},{5,7},{6,4},{7,5},{8,10},{9,11},{10,... | collective-permute-start | bytes 393224 | tf_op jit(solution)/shard_map/ppermute | solution.py:282
  6.2 0.0 slice-done
  6.2 0.0 slice-done.1
  6.2 0.0 copy-done.1
  6.2 2.1 %shard_map.76 = (f32[64,512]{1,0:T(8,128)S(1)}, f32[64,512]{1,0:T(8,128)S(1)}) custom-call(bf16[64,3584]{1,0:T(8,128)(2,1)S(1)} %copy-done.1, bf16[2,512,3584]{2,1,0:T(8,128)(2,1)S(1)} %bitcast.2, f32[64,512]{1,0:T(8,128)S(1)} %shard_map.75.after_ref.out_chip_ref), custom_call_target="tpu_custom_call" | custom-call | flops 939524096 | bytes 7340032 | tf_op jit(solution)/shard_map/pallas_call | solution.py:112
  8.3 0.1 collective-permute-start.1
  8.4 0.0 copy-done
  8.4 0.5 %shard_map.77.after_ref.norm_ref = f32[1,1024]{1,0:T(1,128)S(1)} custom-call(bf16[1024,1024]{1,0:T(8,128)(2,1)S(1)} %copy-done, f32[64,512]{1,0:T(8,128)S(1)} %get-tuple-element.18.after_ref), custom_call_target="tpu_custom_call" | custom-call | flops 2097152 | bytes 2097152 | tf_op jit(solution)/shard_map/pallas_call | solution.py:171
  8.9 1.1 %collective-permute-done.2.out_got_ref = f32[64,512]{1,0:T(8,128)S(1)} collective-permute-done((f32[64,512]{1,0:T(8,128)S(1)}, f32[64,512]{1,0:T(8,128)S(1)}, u32[]{:S(2)}, u32[]{:S(2)}) %collective-permute-start.2) | collective-permute-done | bytes 131104 | tf_op jit(solution)/shard_map/ppermute | solution.py:282
  10.0 0.0 collective-permute-done.1.in_got_ref
  10.0 0.3 %shard_map.78 = f32[32,8,128]{2,1,0:T(8,128)S(1)} custom-call(f32[1,512]{1,0:T(1,128)S(1)} %bitcast.4, f32[64,512]{1,0:T(8,128)S(1)} %get-tuple-element.17.in_keep_ref, f32[64,512]{1,0:T(8,128)S(1)} %collective-permute-done.1.in_got_ref, f32[64,512]{1,0:T(8,128)S(1)} %shard_map.75.after_ref.out_chip_ref, f32[64,512]{1,0:T(8,128)S(1)} %collective-permute-done.2.out_got_ref, ...), custom_call_target="tpu_custom_call" | custom-call | flops 25165824 | bytes 131072 | tf_op jit(solution)/shard_map/pallas_call | solution.py:146
  10.4 14.4 %all_to_all.5.partials_ref = f32[32,8,128]{2,1,0:T(8,128)S(1)} all-to-all(f32[32,8,128]{2,1,0:T(8,128)S(1)} %shard_map.78), channel_id=1, replica_groups=mesh['bank'=8,'tp'=4] {'bank','tp'}, dimensions={0} | all-to-all | bytes 262144 | tf_op jit(solution)/shard_map/all_to_all | solution.py:287
  24.8 0.8 %shard_map.79 = (f32[3,1152]{1,0:T(4,128)S(1)}, f32[3,1152]{1,0:T(4,128)S(1)}, f32[3,1152]{1,0:T(4,128)S(1)}, f32[3,1152]{1,0:T(4,128)S(1)}) custom-call(f32[8,32]{1,0:T(8,128)S(1)} %multiply_reduce_fusion.refs_1_.signs_ref, f32[32,8,128]{2,1,0:T(8,128)S(1)} %all_to_all.5.partials_ref, bf16[1024,1024]{1,0:T(8,128)(2,1)S(1)} %copy-done, ...), custom_call_target="tpu_custom_call" | custom-call | flops 16777216 | bytes 2097152 | tf_op jit(solution)/shard_map/pallas_call | solution.py:215
  25.6 0.2 collective-permute-start.3
  25.8 0.4 %collective-permute-start.4 = (f32[3,1152]{1,0:T(4,128)S(1)}, f32[3,1152]{1,0:T(4,128)S(1)}, u32[]{:S(2)}, u32[]{:S(2)}) collective-permute-start(f32[3,1152]{1,0:T(4,128)S(1)} %get-tuple-element.21), channel_id=1, source_target_pairs={{0,2},{1,3},{2,0},{3,1},{4,6},{5,7},{6,4},{7,5},{8,10},{9,11},{10,... | collective-permute-start | bytes 41480 | tf_op jit(solution)/shard_map/ppermute | solution.py:289
  26.2 1.3 %collective-permute-start.5 = (f32[3,1152]{1,0:T(4,128)S(1)}, f32[3,1152]{1,0:T(4,128)S(1)}, u32[]{:S(2)}, u32[]{:S(2)}) collective-permute-start(f32[3,1152]{1,0:T(4,128)S(1)} %get-tuple-element.22), channel_id=1, source_target_pairs={{0,3},{1,2},{2,1},{3,0},{4,7},{5,6},{6,5},{7,4},{8,11},{9,10},{10,... | collective-permute-start | bytes 41480 | tf_op jit(solution)/shard_map/ppermute | solution.py:289
  27.5 0.0 collective-permute-done.3.refs_0_
  27.5 2.1 %collective-permute-done.4.refs_1_ = f32[3,1152]{1,0:T(4,128)S(1)} collective-permute-done((f32[3,1152]{1,0:T(4,128)S(1)}, f32[3,1152]{1,0:T(4,128)S(1)}, u32[]{:S(2)}, u32[]{:S(2)}) %collective-permute-start.4) | collective-permute-done | bytes 13856 | tf_op jit(solution)/shard_map/ppermute | solution.py:289
  29.6 0.0 collective-permute-done.5.refs_2_
  29.6 0.7 %shard_map.80 = f32[2,1024]{1,0:T(2,128)} custom-call(f32[3,1152]{1,0:T(4,128)S(1)} %get-tuple-element.19.own_ref, f32[3,1152]{1,0:T(4,128)S(1)} %collective-permute-done.3.refs_0_, f32[3,1152]{1,0:T(4,128)S(1)} %collective-permute-done.4.refs_1_, f32[3,1152]{1,0:T(4,128)S(1)} %collective-permute-done.5.refs_2_), custom_call_target="tpu_custom_call" | custom-call | tf_op jit(solution)/shard_map/pallas_call | solution.py:256
  (5 shorter events, 0.0 us)
Async XLA Ops:
  0.0 2.4 %copy-start.2 = (s32[16]{0:T(128)S(1)}, s32[16]{0:T(128)}, u32[]{:S(2)}) copy-start(s32[16]{0:T(128)} %param.12) | copy-start | bytes 196
  0.0 3.0 %copy-start.3 = (s32[2]{0:T(128)S(1)}, s32[2]{0:T(128)}, u32[]{:S(2)}) copy-start(s32[2]{0:T(128)} %param.11) | copy-start | bytes 28
  1.8 1.5 %collective-permute-start = (f32[64,512]{1,0:T(8,128)S(1)}, f32[64,512]{1,0:T(8,128)S(1)}, u32[]{:S(2)}, u32[]{:S(2)}) collective-permute-start(f32[64,512]{1,0:T(8,128)S(1)} %get-tuple-element.16), channel_id=1, source_target_pairs={{0,1},{1,0},{2,3},{3,2},{4,5},{5,4},{6,7},{7,6},{8,9},{9,8},{10,11... | collective-permute-start | bytes 393224 | tf_op jit(solution)/shard_map/ppermute | solution.py:280
  2.6 3.7 %slice-start = ((s8[7340032]{0:T(1024)(128)(4,1)}), s8[3145728]{0:T(1024)(128)(4,1)S(1)}, s32[]{:S(2)}) async-start(s8[7340032]{0:T(1024)(128)(4,1)} %bitcast.1), calls=%async_computation.1 | async-start | bytes 6291456
  3.3 3.0 %slice-start.1 = ((s8[7340032]{0:T(1024)(128)(4,1)}), s8[4194304]{0:T(1024)(128)(4,1)S(1)}, s32[]{:S(2)}) async-start(s8[7340032]{0:T(1024)(128)(4,1)} %bitcast.1), calls=%async_computation.2 | async-start | bytes 8388608
  3.3 3.0 %copy-start.1 = (bf16[64,3584]{1,0:T(8,128)(2,1)S(1)}, bf16[64,3584]{1,0:T(8,128)(2,1)}, u32[]{:S(2)}) copy-start(bf16[64,3584]{1,0:T(8,128)(2,1)} %proj_ref.3) | copy-start | bytes 1376260
  3.3 5.1 %copy-start = (bf16[1024,1024]{1,0:T(8,128)(2,1)S(1)}, bf16[1024,1024]{1,0:T(8,128)(2,1)}, u32[]{:S(2)}) copy-start(bf16[1024,1024]{1,0:T(8,128)(2,1)} %slab_ref.3) | copy-start | bytes 6291460
  3.3 6.7 %collective-permute-start.2 = (f32[64,512]{1,0:T(8,128)S(1)}, f32[64,512]{1,0:T(8,128)S(1)}, u32[]{:S(2)}, u32[]{:S(2)}) collective-permute-start(f32[64,512]{1,0:T(8,128)S(1)} %shard_map.75.after_ref.out_chip_ref), channel_id=1, source_target_pairs={{0,2},{1,3},{2,0},{3,1},{4,6},{5,7},{6,4},{7,5},{8,10},{9,11},{10,... | collective-permute-start | bytes 393224 | tf_op jit(solution)/shard_map/ppermute | solution.py:282
  8.3 1.7 %collective-permute-start.1 = (f32[64,512]{1,0:T(8,128)S(1)}, f32[64,512]{1,0:T(8,128)S(1)}, u32[]{:S(2)}, u32[]{:S(2)}) collective-permute-start(f32[64,512]{1,0:T(8,128)S(1)} %get-tuple-element.18.after_ref), channel_id=1, source_target_pairs={{0,1},{1,0},{2,3},{3,2},{4,5},{5,4},{6,7},{7,6},{8,9},{9,8},{10,11... | collective-permute-start | bytes 393224 | tf_op jit(solution)/shard_map/ppermute | solution.py:284
  25.6 1.9 %collective-permute-start.3 = (f32[3,1152]{1,0:T(4,128)S(1)}, f32[3,1152]{1,0:T(4,128)S(1)}, u32[]{:S(2)}, u32[]{:S(2)}) collective-permute-start(f32[3,1152]{1,0:T(4,128)S(1)} %get-tuple-element.20), channel_id=1, source_target_pairs={{0,1},{1,0},{2,3},{3,2},{4,5},{5,4},{6,7},{7,6},{8,9},{9,8},{10,11... | collective-permute-start | bytes 41480 | tf_op jit(solution)/shard_map/ppermute | solution.py:289
  25.8 3.8 %collective-permute-start.4 = (f32[3,1152]{1,0:T(4,128)S(1)}, f32[3,1152]{1,0:T(4,128)S(1)}, u32[]{:S(2)}, u32[]{:S(2)}) collective-permute-start(f32[3,1152]{1,0:T(4,128)S(1)} %get-tuple-element.21), channel_id=1, source_target_pairs={{0,2},{1,3},{2,0},{3,1},{4,6},{5,7},{6,4},{7,5},{8,10},{9,11},{10,... | collective-permute-start | bytes 41480 | tf_op jit(solution)/shard_map/ppermute | solution.py:289
  26.2 3.4 %collective-permute-start.5 = (f32[3,1152]{1,0:T(4,128)S(1)}, f32[3,1152]{1,0:T(4,128)S(1)}, u32[]{:S(2)}, u32[]{:S(2)}) collective-permute-start(f32[3,1152]{1,0:T(4,128)S(1)} %get-tuple-element.22), channel_id=1, source_target_pairs={{0,3},{1,2},{2,1},{3,0},{4,7},{5,6},{6,5},{7,4},{8,11},{9,10},{10,... | collective-permute-start | bytes 41480 | tf_op jit(solution)/shard_map/ppermute | solution.py:289

commit v4 on v3

--- a/solution.py
+++ b/solution.py
@@ -27,39 +27,68 @@
     return pltpu.with_memory_space_constraint(arr, pltpu.HBM)
 
 
-def out_send_kernel(proj_ref, rows_ref, send_ref, proj_held, rows_held, rows_buf, sems):
-    core = lax.rem(lax.axis_index("tp"), 2)
+def out_send_kernel(
+    pairs_mine, proj_ref, rows_ref, lengths_ref, perm_ref,
+    send_ref, proj_held, rows_held, live_ref, signs_ref,
+    rows_buf, lengths_buf, perm_buf, sems,
+):
+    k = lax.axis_index("tp")
+    core = lax.rem(k, 2)
     copies = [
-        pltpu.make_async_copy(rows_ref.at[1 - core], rows_buf, sems.at[0]),
-        pltpu.make_async_copy(proj_ref, proj_held, sems.at[1]),
-        pltpu.make_async_copy(rows_ref.at[core], rows_held, sems.at[2]),
+        pltpu.make_async_copy(perm_ref, perm_buf, sems.at[0]),
+        pltpu.make_async_copy(lengths_ref, lengths_buf, sems.at[1]),
+        pltpu.make_async_copy(rows_ref.at[1 - core], rows_buf, sems.at[2]),
+        pltpu.make_async_copy(proj_ref, proj_held, sems.at[3]),
+        pltpu.make_async_copy(rows_ref.at[core], rows_held, sems.at[4]),
     ]
     for copy in copies:
         copy.start()
     copies[0].wait()
     copies[1].wait()
+    position = lax.broadcasted_iota(jnp.int32, live_ref.shape, 1)
+    live_ref[...] = (position < lengths_buf[core]).astype(jnp.float32)
+    row = lax.broadcasted_iota(jnp.int32, signs_ref.shape, 0)
+    source = lax.broadcasted_iota(jnp.int32, signs_ref.shape, 1)
+    example = (source // 4) * 2 + source % 2
+    signs = jnp.zeros(signs_ref.shape, jnp.float32)
+    for slot in range(perm_ref.shape[0]):
+        pair = slot // 2
+        place = ((pair // pairs_mine) ^ k) * pairs_mine + pair % pairs_mine
+        hit = (row == place) & (example == perm_buf[slot])
+        signs = jnp.where(hit, 1.0 if slot % 2 else -1.0, signs)
+    signs_ref[...] = signs
+    copies[2].wait()
+    copies[3].wait()
     put_factor(rows_buf[...], proj_held[...], send_ref, 0)
-    copies[2].wait()
-
-
-def out_send(proj, rows):
+    copies[4].wait()
+
+
+def out_send(proj, rows, lengths, pair_perm, sources, tp_count):
     rank, depth = proj.shape
     _, tokens, _ = rows.shape
-    return pl.pallas_call(
-        out_send_kernel,
+    pair_count = pair_perm.shape[0] // 2
+    return pl.pallas_call(
+        functools.partial(out_send_kernel, pair_count // tp_count),
         out_shape=[
             jax.ShapeDtypeStruct((rank, tokens), jnp.float32),
             jax.ShapeDtypeStruct(proj.shape, proj.dtype),
             jax.ShapeDtypeStruct((tokens, depth), rows.dtype),
+            jax.ShapeDtypeStruct((1, tokens), jnp.float32),
+            jax.ShapeDtypeStruct((pair_count, sources), jnp.float32),
         ],
-        in_specs=[ANY, ANY],
-        out_specs=[VMEM, VMEM, VMEM],
-        scratch_shapes=[pltpu.VMEM((tokens, depth), rows.dtype), pltpu.SemaphoreType.DMA((3,))],
+        in_specs=[ANY] * 4,
+        out_specs=[VMEM] * 5,
+        scratch_shapes=[
+            pltpu.VMEM((tokens, depth), rows.dtype),
+            pltpu.SMEM(lengths.shape, lengths.dtype),
+            pltpu.SMEM(pair_perm.shape, pair_perm.dtype),
+            pltpu.SemaphoreType.DMA((5,)),
+        ],
         compiler_params=pltpu.CompilerParams(vmem_limit_bytes=8 << 20),
         cost_estimate=pl.CostEstimate(
             flops=4 * rank * depth * tokens, bytes_accessed=4 * depth * tokens, transcendentals=0
         ),
-    )(in_hbm(proj), in_hbm(rows))
+    )(in_hbm(proj), in_hbm(rows), in_hbm(lengths), in_hbm(pair_perm))
 
 
 def out_keep_kernel(proj_ref, rows_ref, out_ref):
@@ -76,25 +105,24 @@
         out_specs=VMEM,
         compiler_params=pltpu.CompilerParams(vmem_limit_bytes=8 << 20),
         cost_estimate=pl.CostEstimate(
-            flops=4 * rank * depth * tokens, bytes_accessed=2 * depth * tokens, transcendentals=0
+            flops=4 * 10**9, bytes_accessed=2 * depth * tokens, transcendentals=0
         ),
     )(proj, rows)
 
 
-def add_kernel(left_ref, right_ref, *refs):
-    out_ref = refs[-1]
+def add_kernel(left_ref, right_ref, out_ref):
     out_ref[...] = left_ref[...] + right_ref[...]
 
 
-def add(left, right, *after):
+def add(left, right, flops):
     return pl.pallas_call(
         add_kernel,
         out_shape=jax.ShapeDtypeStruct(left.shape, left.dtype),
-        in_specs=[VMEM, VMEM] + [ANY] * len(after),
+        in_specs=[VMEM, VMEM],
         out_specs=VMEM,
         compiler_params=pltpu.CompilerParams(vmem_limit_bytes=4 << 20),
-        cost_estimate=pl.CostEstimate(flops=4 * 10**9, bytes_accessed=16 << 20, transcendentals=0),
-    )(left, right, *after)
+        cost_estimate=pl.CostEstimate(flops=flops, bytes_accessed=16 << 20, transcendentals=0),
+    )(left, right)
 
 
 def in_kernel(proj_ref, rows_ref, after_ref, send_ref, keep_ref):
@@ -121,13 +149,12 @@
     )(proj, rows, after)
 
 
-def outer_kernel(live_ref, in_keep_ref, in_got_ref, out_chip_ref, out_got_ref, after_ref, send_ref, grads_ref):
+def outer_kernel(live_ref, in_keep_ref, in_got_ref, out_full_ref, after_ref, send_ref, grads_ref):
     rank = in_keep_ref.shape[0]
     masked = jnp.where(live_ref[...] > 0.0, in_keep_ref[...] + in_got_ref[...], 0.0)
-    out_full = out_chip_ref[...] + out_got_ref[...]
     grads_ref[...] = lax.dot_general(
         masked,
-        out_full,
+        out_full_ref[...],
         (((1,), (1,)), ((), ())),
         precision=lax.Precision.HIGHEST,
         preferred_element_type=jnp.float32,
@@ -141,19 +168,19 @@
         send_ref[target] = packed[share * 8 : share * 8 + 8, :]
 
 
-def outer(live, in_keep, in_got, out_chip, out_got, after, targets):
+def outer(live, in_keep, in_got, out_full, after, targets):
     rank, tokens = in_keep.shape
     return pl.pallas_call(
         outer_kernel,
         out_shape=jax.ShapeDtypeStruct((targets, rank // 8, 2 * rank), jnp.float32),
-        in_specs=[VMEM, VMEM, VMEM, VMEM, VMEM, ANY],
+        in_specs=[VMEM] * 4 + [ANY],
         out_specs=VMEM,
         scratch_shapes=[pltpu.VMEM((rank, rank), jnp.float32)],
         compiler_params=pltpu.CompilerParams(vmem_limit_bytes=8 << 20),
         cost_estimate=pl.CostEstimate(
             flops=12 * rank * rank * tokens, bytes_accessed=4 * rank * tokens, transcendentals=0
         ),
-    )(live, in_keep, in_got, out_chip, out_got, after)
+    )(live, in_keep, in_got, out_full, after)
 
 
 def norm_kernel(slab_ref, after_ref, out_ref):
@@ -224,21 +251,6 @@
     )(signs, partials, slab, bank_part)
 
 
-def pair_signs(pair_perm, sources, tp_count):
-    slots = jnp.arange(pair_perm.shape[0], dtype=jnp.int32)
-    pair_count = pair_perm.shape[0] // 2
-    pairs_mine = pair_count // tp_count
-    order = jnp.arange(pair_count, dtype=jnp.int32)
-    pair = ((order // pairs_mine) ^ lax.axis_index("tp")) * pairs_mine + order % pairs_mine
-    weights = (slots[None, :] == 2 * pair[:, None] + 1).astype(jnp.float32) - (
-        slots[None, :] == 2 * pair[:, None]
-    ).astype(jnp.float32)
-    source = jnp.arange(sources, dtype=jnp.int32)
-    example = (source // tp_count) * 2 + source % 2
-    hits = (pair_perm[None, :, None] == example[None, None, :]).astype(jnp.float32)
-    return jnp.sum(weights[:, :, None] * hits, axis=1)
-
-
 def scores_kernel(scale, own_ref, *refs):
     *got_refs, out_ref = refs
     total = own_ref[...]
@@ -262,28 +274,21 @@
     )(*messages)
 
 
-def live_row(lengths, tokens):
-    prompts = jnp.arange(lengths.shape[0], dtype=jnp.int32)
-    positions = jnp.arange(tokens, dtype=jnp.int32)
-    mine = prompts == lax.rem(lax.axis_index("tp"), 2)
-    live = mine[:, None] & (positions[None, :] < lengths[:, None])
-    return jnp.sum(live.astype(jnp.float32), axis=0, keepdims=True)
-
-
 def per_device(hidden, out_grad, proj_in, proj_out, lengths, pair_perm, bank_slab):
     rank = proj_in.shape[0]
     tp_count = lax.axis_size("tp")
     bank_count = lax.axis_size("bank")
-    live = live_row(lengths, hidden.shape[1])
-    signs = pair_signs(pair_perm, bank_count * tp_count, tp_count)
-    out_away, proj_held, rows_held = out_send(proj_out, out_grad)
+    out_away, proj_held, rows_held, live, signs = out_send(
+        proj_out, out_grad, lengths, pair_perm, bank_count * tp_count, tp_count
+    )
     out_got = lax.ppermute(out_away, "tp", flip(1))
-    out_chip = add(out_keep(proj_held, rows_held), out_got, live, signs)
+    out_chip = add(out_keep(proj_held, rows_held), out_got, 4)
     out_other = lax.ppermute(out_chip, "tp", flip(2))
     in_away, in_keep = in_factors(proj_in, hidden, out_chip)
     in_got = lax.ppermute(in_away, "tp", flip(1))
+    out_full = add(out_chip, out_other, 4 * 10**9)
     bank_part = norms(bank_slab, in_away)
-    outgoing = outer(live, in_keep, in_got, out_chip, out_other, bank_part, bank_count * tp_count)
+    outgoing = outer(live, in_keep, in_got, out_full, bank_part, bank_count * tp_count)
     partials = lax.all_to_all(outgoing, ("bank", "tp"), 0, 0, tiled=True)
     messages = dots(signs, partials, bank_slab, bank_part, tp_count)
     got = [messages[0]] + [lax.ppermute(messages[step], "tp", flip(step)) for step in range(1, 4)]

time: 30.4 us -> 30.1 us (level)
  waiting for transfers between devices: 3.37 us -> 3.77 us
  other arithmetic: 0.35 us -> 0.01 us
    ppermute x1, waiting for transfers between devices: 0.13 us -> 0.52 us  [per_device(): out_got = lax.ppermute(out_away, 'tp', flip(1))]
  transfers between devices with their start and end apart: 6 -> 6, of which waited for: 3 -> 3; matrix products, arithmetic and copies ran while one was open for 1% -> 0% of each run, Pallas kernels for 10% -> 10%
where the time goes in v4:
time: 30.1 us; the launch traced here: 30 us
  blocking collectives  14.1 us (47%)
  Pallas kernels  6.6 us (22%)
  starting transfers between devices  5.38 us (18%)
  waiting for transfers between devices  3.77 us (13%)
    all_to_all x1, blocking collectives, per_device(): partials = lax.all_to_all(outgoing, ('bank', 'tp'), 0, 0, tiled=True)  14.1 us
    ppermute x1, starting transfers between devices, per_device(): out_other = lax.ppermute(out_chip, 'tp', flip(2))  2.91 us
    ppermute x3, waiting for transfers between devices, per_device(): lax.ppermute(messages[step], 'tp', flip(step))  2.12 us
    pallas_call x1, Pallas kernels, in_factors(): pl.pallas_call(in_kernel, out_shape=[jax.ShapeDtypeStruct((rank, tokens),...  2.11 us
    ppermute x3, starting transfers between devices, per_device(): lax.ppermute(messages[step], 'tp', flip(step))  1.88 us
    pallas_call x1, Pallas kernels, out_send(): pl.pallas_call(functools.partial(out_send_kernel, pair_count // tp_count)...  1.74 us
    ppermute x1, waiting for transfers between devices, per_device(): out_other = lax.ppermute(out_chip, 'tp', flip(2))  1.13 us
    pallas_call x1, Pallas kernels, dots(): pl.pallas_call(dots_kernel, out_shape=[message] * tp_count, in_specs=[VME...  0.77 us
  transfers between devices with their start and end apart: 6, of which 3 were waited for; matrix products, arithmetic and copies ran while one was open for 0% of the time, Pallas kernels for 10%

profile of v4, /device:TPU:0, one launch (start us, length us, event | category | flops | bytes accessed | tf_op | source)
XLA Modules:
  0.0 30.0 jit_solution(6613200879892775938)
XLA Ops:
  0.0 1.7 %shard_map.73 = (f32[64,512]{1,0:T(8,128)S(1)}, bf16[64,1024]{1,0:T(8,128)(2,1)S(1)}, bf16[512,1024]{1,0:T(8,128)(2,1)S(1)}, f32[1,512]{1,0:T(1,128)S(1)}, f32[8,32]{1,0:T(8,128)S(1)}) custom-call(bf16[64,1024]{1,0:T(8,128)(2,1)} %proj_ref.2, bf16[2,512,1024]{2,1,0:T(8,128)(2,1)} %rows_ref.2, s32[2]{0:T(128)} %lengths_ref.1, s32[16]{0:T(128)} %perm_ref.1), custom_call_target="tpu_custom_call" | custom-call | flops 134217728 | bytes 2097152 | tf_op jit(solution)/shard_map/pallas_call | solution.py:70
  1.7 0.5 %collective-permute-start = (f32[64,512]{1,0:T(8,128)S(1)}, f32[64,512]{1,0:T(8,128)S(1)}, u32[]{:S(2)}, u32[]{:S(2)}) collective-permute-start(f32[64,512]{1,0:T(8,128)S(1)} %get-tuple-element.20), channel_id=1, source_target_pairs={{0,1},{1,0},{2,3},{3,2},{4,5},{5,4},{6,7},{7,6},{8,9},{9,8},{10,11... | collective-permute-start | bytes 393224 | tf_op jit(solution)/shard_map/ppermute | solution.py:284
  2.3 0.0 slice-start
  2.3 0.0 slice-start.1
  2.3 0.0 copy-start.1
  2.3 0.5 %shard_map.74.left_ref = f32[64,512]{1,0:T(8,128)S(1)} custom-call(bf16[64,1024]{1,0:T(8,128)(2,1)S(1)} %get-tuple-element.18.proj_ref, bf16[512,1024]{1,0:T(8,128)(2,1)S(1)} %get-tuple-element.19.rows_ref), custom_call_target="tpu_custom_call" | custom-call | flops 4000000000 | bytes 1048576 | tf_op jit(solution)/shard_map/pallas_call | solution.py:101
  2.7 0.5 %collective-permute-done.right_ref = f32[64,512]{1,0:T(8,128)S(1)} collective-permute-done((f32[64,512]{1,0:T(8,128)S(1)}, f32[64,512]{1,0:T(8,128)S(1)}, u32[]{:S(2)}, u32[]{:S(2)}) %collective-permute-start) | collective-permute-done | bytes 131104 | tf_op jit(solution)/shard_map/ppermute | solution.py:284
  3.3 0.0 copy-start
  3.3 2.9 %collective-permute-start.2 = (f32[64,512]{1,0:T(8,128)S(1)}, f32[64,512]{1,0:T(8,128)S(1)}, u32[]{:S(2)}, u32[]{:S(2)}) collective-permute-start(f32[64,512]{1,0:T(8,128)S(1)} %shard_map.75.after_ref.left_ref), channel_id=1, source_target_pairs={{0,2},{1,3},{2,0},{3,1},{4,6},{5,7},{6,4},{7,5},{8,10},{9,11},{10,... | collective-permute-start | bytes 393224 | tf_op jit(solution)/shard_map/ppermute | solution.py:286
  6.2 0.0 slice-done
  6.2 0.0 slice-done.1
  6.2 0.0 copy-done.1
  6.2 2.1 %shard_map.76 = (f32[64,512]{1,0:T(8,128)S(1)}, f32[64,512]{1,0:T(8,128)S(1)}) custom-call(bf16[64,3584]{1,0:T(8,128)(2,1)S(1)} %copy-done.1, bf16[2,512,3584]{2,1,0:T(8,128)(2,1)S(1)} %bitcast.1, f32[64,512]{1,0:T(8,128)S(1)} %shard_map.75.after_ref.left_ref), custom_call_target="tpu_custom_call" | custom-call | flops 939524096 | bytes 7340032 | tf_op jit(solution)/shard_map/pallas_call | solution.py:140
  8.3 0.1 collective-permute-start.1
  8.4 0.0 copy-done
  8.4 0.5 %shard_map.78.after_ref.norm_ref = f32[1,1024]{1,0:T(1,128)S(1)} custom-call(bf16[1024,1024]{1,0:T(8,128)(2,1)S(1)} %copy-done, f32[64,512]{1,0:T(8,128)S(1)} %get-tuple-element.22.after_ref), custom_call_target="tpu_custom_call" | custom-call | flops 2097152 | bytes 2097152 | tf_op jit(solution)/shard_map/pallas_call | solution.py:198
  8.9 1.1 %collective-permute-done.2.right_ref = f32[64,512]{1,0:T(8,128)S(1)} collective-permute-done((f32[64,512]{1,0:T(8,128)S(1)}, f32[64,512]{1,0:T(8,128)S(1)}, u32[]{:S(2)}, u32[]{:S(2)}) %collective-permute-start.2) | collective-permute-done | bytes 131104 | tf_op jit(solution)/shard_map/ppermute | solution.py:286
  10.0 0.0 collective-permute-done.1.in_got_ref
  10.0 0.3 %shard_map.79 = f32[32,8,128]{2,1,0:T(8,128)S(1)} custom-call(f32[1,512]{1,0:T(1,128)S(1)} %get-tuple-element.17.live_ref, f32[64,512]{1,0:T(8,128)S(1)} %get-tuple-element.21.in_keep_ref, f32[64,512]{1,0:T(8,128)S(1)} %collective-permute-done.1.in_got_ref, f32[64,512]{1,0:T(8,128)S(1)} %shard_map.77.out_full_ref, f32[1,1024]{1,0:T(1,128)S(1)} %shard_map.78.after_ref.norm_ref), custom_call_target="tpu_custom_call" | custom-call | flops 25165824 | bytes 131072 | tf_op jit(solution)/shard_map/pallas_call | solution.py:173
  10.4 14.1 %all_to_all.5.partials_ref = f32[32,8,128]{2,1,0:T(8,128)S(1)} all-to-all(f32[32,8,128]{2,1,0:T(8,128)S(1)} %shard_map.79), channel_id=1, replica_groups=mesh['bank'=8,'tp'=4] {'bank','tp'}, dimensions={0} | all-to-all | bytes 262144 | tf_op jit(solution)/shard_map/all_to_all | solution.py:292
  24.5 0.8 %shard_map.80 = (f32[3,1152]{1,0:T(4,128)S(1)}, f32[3,1152]{1,0:T(4,128)S(1)}, f32[3,1152]{1,0:T(4,128)S(1)}, f32[3,1152]{1,0:T(4,128)S(1)}) custom-call(f32[8,32]{1,0:T(8,128)S(1)} %get-tuple-element.16.signs_ref, f32[32,8,128]{2,1,0:T(8,128)S(1)} %all_to_all.5.partials_ref, bf16[1024,1024]{1,0:T(8,128)(2,1)S(1)} %copy-done, ...), custom_call_target="tpu_custom_call" | custom-call | flops 16777216 | bytes 2097152 | tf_op jit(solution)/shard_map/pallas_call | solution.py:242
  25.3 0.2 collective-permute-start.3
  25.5 0.4 %collective-permute-start.4 = (f32[3,1152]{1,0:T(4,128)S(1)}, f32[3,1152]{1,0:T(4,128)S(1)}, u32[]{:S(2)}, u32[]{:S(2)}) collective-permute-start(f32[3,1152]{1,0:T(4,128)S(1)} %get-tuple-element.25), channel_id=1, source_target_pairs={{0,2},{1,3},{2,0},{3,1},{4,6},{5,7},{6,4},{7,5},{8,10},{9,11},{10,... | collective-permute-start | bytes 41480 | tf_op jit(solution)/shard_map/ppermute | solution.py:294
  25.9 1.3 %collective-permute-start.5 = (f32[3,1152]{1,0:T(4,128)S(1)}, f32[3,1152]{1,0:T(4,128)S(1)}, u32[]{:S(2)}, u32[]{:S(2)}) collective-permute-start(f32[3,1152]{1,0:T(4,128)S(1)} %get-tuple-element.26), channel_id=1, source_target_pairs={{0,3},{1,2},{2,1},{3,0},{4,7},{5,6},{6,5},{7,4},{8,11},{9,10},{10,... | collective-permute-start | bytes 41480 | tf_op jit(solution)/shard_map/ppermute | solution.py:294
  27.2 0.0 collective-permute-done.3.refs_0_
  27.2 2.1 %collective-permute-done.4.refs_1_ = f32[3,1152]{1,0:T(4,128)S(1)} collective-permute-done((f32[3,1152]{1,0:T(4,128)S(1)}, f32[3,1152]{1,0:T(4,128)S(1)}, u32[]{:S(2)}, u32[]{:S(2)}) %collective-permute-start.4) | collective-permute-done | bytes 13856 | tf_op jit(solution)/shard_map/ppermute | solution.py:294
  29.3 0.0 collective-permute-done.5.refs_2_
  29.3 0.7 %shard_map.81 = f32[2,1024]{1,0:T(2,128)} custom-call(f32[3,1152]{1,0:T(4,128)S(1)} %get-tuple-element.23.own_ref, f32[3,1152]{1,0:T(4,128)S(1)} %collective-permute-done.3.refs_0_, f32[3,1152]{1,0:T(4,128)S(1)} %collective-permute-done.4.refs_1_, f32[3,1152]{1,0:T(4,128)S(1)} %collective-permute-done.5.refs_2_), custom_call_target="tpu_custom_call" | custom-call | tf_op jit(solution)/shard_map/pallas_call | solution.py:268
  (3 shorter events, 0.0 us)
Async XLA Ops:
  1.7 1.5 %collective-permute-start = (f32[64,512]{1,0:T(8,128)S(1)}, f32[64,512]{1,0:T(8,128)S(1)}, u32[]{:S(2)}, u32[]{:S(2)}) collective-permute-start(f32[64,512]{1,0:T(8,128)S(1)} %get-tuple-element.20), channel_id=1, source_target_pairs={{0,1},{1,0},{2,3},{3,2},{4,5},{5,4},{6,7},{7,6},{8,9},{9,8},{10,11... | collective-permute-start | bytes 393224 | tf_op jit(solution)/shard_map/ppermute | solution.py:284
  2.3 3.9 %slice-start = ((s8[7340032]{0:T(1024)(128)(4,1)}), s8[4194304]{0:T(1024)(128)(4,1)S(1)}, s32[]{:S(2)}) async-start(s8[7340032]{0:T(1024)(128)(4,1)} %bitcast), calls=%async_computation.1 | async-start | bytes 8388608
  2.3 3.9 %slice-start.1 = ((s8[7340032]{0:T(1024)(128)(4,1)}), s8[3145728]{0:T(1024)(128)(4,1)S(1)}, s32[]{:S(2)}) async-start(s8[7340032]{0:T(1024)(128)(4,1)} %bitcast), calls=%async_computation.2 | async-start | bytes 6291456
  2.3 3.9 %copy-start.1 = (bf16[64,3584]{1,0:T(8,128)(2,1)S(1)}, bf16[64,3584]{1,0:T(8,128)(2,1)}, u32[]{:S(2)}) copy-start(bf16[64,3584]{1,0:T(8,128)(2,1)} %proj_ref.3) | copy-start | bytes 1376260
  3.3 5.1 %copy-start = (bf16[1024,1024]{1,0:T(8,128)(2,1)S(1)}, bf16[1024,1024]{1,0:T(8,128)(2,1)}, u32[]{:S(2)}) copy-start(bf16[1024,1024]{1,0:T(8,128)(2,1)} %slab_ref.3) | copy-start | bytes 6291460
  3.3 6.7 %collective-permute-start.2 = (f32[64,512]{1,0:T(8,128)S(1)}, f32[64,512]{1,0:T(8,128)S(1)}, u32[]{:S(2)}, u32[]{:S(2)}) collective-permute-start(f32[64,512]{1,0:T(8,128)S(1)} %shard_map.75.after_ref.left_ref), channel_id=1, source_target_pairs={{0,2},{1,3},{2,0},{3,1},{4,6},{5,7},{6,4},{7,5},{8,10},{9,11},{10,... | collective-permute-start | bytes 393224 | tf_op jit(solution)/shard_map/ppermute | solution.py:286
  8.3 1.7 %collective-permute-start.1 = (f32[64,512]{1,0:T(8,128)S(1)}, f32[64,512]{1,0:T(8,128)S(1)}, u32[]{:S(2)}, u32[]{:S(2)}) collective-permute-start(f32[64,512]{1,0:T(8,128)S(1)} %get-tuple-element.22.after_ref), channel_id=1, source_target_pairs={{0,1},{1,0},{2,3},{3,2},{4,5},{5,4},{6,7},{7,6},{8,9},{9,8},{10,11... | collective-permute-start | bytes 393224 | tf_op jit(solution)/shard_map/ppermute | solution.py:288
  25.3 1.9 %collective-permute-start.3 = (f32[3,1152]{1,0:T(4,128)S(1)}, f32[3,1152]{1,0:T(4,128)S(1)}, u32[]{:S(2)}, u32[]{:S(2)}) collective-permute-start(f32[3,1152]{1,0:T(4,128)S(1)} %get-tuple-element.24), channel_id=1, source_target_pairs={{0,1},{1,0},{2,3},{3,2},{4,5},{5,4},{6,7},{7,6},{8,9},{9,8},{10,11... | collective-permute-start | bytes 41480 | tf_op jit(solution)/shard_map/ppermute | solution.py:294
  25.5 3.8 %collective-permute-start.4 = (f32[3,1152]{1,0:T(4,128)S(1)}, f32[3,1152]{1,0:T(4,128)S(1)}, u32[]{:S(2)}, u32[]{:S(2)}) collective-permute-start(f32[3,1152]{1,0:T(4,128)S(1)} %get-tuple-element.25), channel_id=1, source_target_pairs={{0,2},{1,3},{2,0},{3,1},{4,6},{5,7},{6,4},{7,5},{8,10},{9,11},{10,... | collective-permute-start | bytes 41480 | tf_op jit(solution)/shard_map/ppermute | solution.py:294
  25.9 3.4 %collective-permute-start.5 = (f32[3,1152]{1,0:T(4,128)S(1)}, f32[3,1152]{1,0:T(4,128)S(1)}, u32[]{:S(2)}, u32[]{:S(2)}) collective-permute-start(f32[3,1152]{1,0:T(4,128)S(1)} %get-tuple-element.26), channel_id=1, source_target_pairs={{0,3},{1,2},{2,1},{3,0},{4,7},{5,6},{6,5},{7,4},{8,11},{9,10},{10,... | collective-permute-start | bytes 41480 | tf_op jit(solution)/shard_map/ppermute | solution.py:294

commit v5 on v4

--- a/solution.py
+++ b/solution.py
@@ -14,6 +14,17 @@
 
 def flip(step):
     return [(i, i ^ step) for i in range(4)]
+
+
+def exchange_order(bank_count):
+    far = bank_count // 2
+    return [
+        ((far - 1 - high) * 2 + low) * 4 + chip * 2 + core
+        for chip in range(2)
+        for low in range(2)
+        for core in range(2)
+        for high in range(far)
+    ]
 
 
 def put_factor(rows, proj, out_ref, start):
@@ -49,7 +60,9 @@
     live_ref[...] = (position < lengths_buf[core]).astype(jnp.float32)
     row = lax.broadcasted_iota(jnp.int32, signs_ref.shape, 0)
     source = lax.broadcasted_iota(jnp.int32, signs_ref.shape, 1)
-    example = (source // 4) * 2 + source % 2
+    far = signs_ref.shape[1] // 8
+    bank = (far - 1 - source % far) * 2 + (source // (2 * far)) % 2
+    example = bank * 2 + (source // far) % 2
     signs = jnp.zeros(signs_ref.shape, jnp.float32)
     for slot in range(perm_ref.shape[0]):
         pair = slot // 2
@@ -125,31 +138,29 @@
     )(left, right)
 
 
-def in_kernel(proj_ref, rows_ref, after_ref, send_ref, keep_ref):
-    core = lax.rem(lax.axis_index("tp"), 2)
+def in_kernel(swap, proj_ref, rows_ref, after_ref, out_ref):
+    prompt = lax.rem(lax.axis_index("tp") + swap, 2)
     tokens = rows_ref.shape[1]
-    for swap, out_ref in ((1, send_ref), (0, keep_ref)):
-        prompt = lax.rem(core + swap, 2)
-        for start in range(0, tokens, 256):
-            put_factor(rows_ref[prompt, start : start + 256, :], proj_ref[...], out_ref, start)
-
-
-def in_factors(proj, rows, after):
+    for start in range(0, tokens, 256):
+        put_factor(rows_ref[prompt, start : start + 256, :], proj_ref[...], out_ref, start)
+
+
+def in_factor(proj, rows, after, swap):
     rank, depth = proj.shape
     tokens = rows.shape[1]
     return pl.pallas_call(
-        in_kernel,
-        out_shape=[jax.ShapeDtypeStruct((rank, tokens), jnp.float32)] * 2,
+        functools.partial(in_kernel, swap),
+        out_shape=jax.ShapeDtypeStruct((rank, tokens), jnp.float32),
         in_specs=[VMEM, VMEM, ANY],
-        out_specs=[VMEM, VMEM],
-        compiler_params=pltpu.CompilerParams(vmem_limit_bytes=8 << 20),
-        cost_estimate=pl.CostEstimate(
-            flops=8 * rank * depth * tokens, bytes_accessed=4 * depth * tokens, transcendentals=0
+        out_specs=VMEM,
+        compiler_params=pltpu.CompilerParams(vmem_limit_bytes=8 << 20),
+        cost_estimate=pl.CostEstimate(
+            flops=4 * rank * depth * tokens, bytes_accessed=2 * depth * tokens, transcendentals=0
         ),
     )(proj, rows, after)
 
 
-def outer_kernel(live_ref, in_keep_ref, in_got_ref, out_full_ref, after_ref, send_ref, grads_ref):
+def outer_kernel(shares, live_ref, in_keep_ref, in_got_ref, out_full_ref, after_ref, send_ref, grads_ref):
     rank = in_keep_ref.shape[0]
     masked = jnp.where(live_ref[...] > 0.0, in_keep_ref[...] + in_got_ref[...], 0.0)
     grads_ref[...] = lax.dot_general(
@@ -163,16 +174,15 @@
     even = grads_ref[pl.ds(0, half, stride=2), :]
     odd = grads_ref[pl.ds(1, half, stride=2), :]
     packed = jnp.concatenate([even, odd], axis=1)
-    for target in range(send_ref.shape[0]):
-        share = target % 4
+    for target, share in enumerate(shares):
         send_ref[target] = packed[share * 8 : share * 8 + 8, :]
 
 
-def outer(live, in_keep, in_got, out_full, after, targets):
+def outer(live, in_keep, in_got, out_full, after, shares):
     rank, tokens = in_keep.shape
     return pl.pallas_call(
-        outer_kernel,
-        out_shape=jax.ShapeDtypeStruct((targets, rank // 8, 2 * rank), jnp.float32),
+        functools.partial(outer_kernel, shares),
+        out_shape=jax.ShapeDtypeStruct((len(shares), rank // 8, 2 * rank), jnp.float32),
         in_specs=[VMEM] * 4 + [ANY],
         out_specs=VMEM,
         scratch_shapes=[pltpu.VMEM((rank, rank), jnp.float32)],
@@ -205,6 +215,10 @@
             flops=2 * rows * cols, bytes_accessed=2 * rows * cols, transcendentals=0
         ),
     )(slab, after)
+
+
+def norm_chunk(rows, pairs_mine):
+    return max(128, rows // pairs_mine)
 
 
 def dots_kernel(signs_ref, partials_ref, slab_ref, norm_ref, *message_refs):
@@ -227,18 +241,23 @@
         (((1,), (1,)), ((), ())),
         preferred_element_type=jnp.float32,
     )
+    chunk = norm_chunk(rows, pairs_mine)
     for step, message_ref in enumerate(message_refs):
         mine = slice(step * pairs_mine, (step + 1) * pairs_mine)
-        message_ref[0:pairs_mine, 0:rows] = dots[mine]
-        message_ref[pairs_mine : pairs_mine + 1, 0:rows] = norm_ref[...]
-        message_ref[0:pairs_mine, rows : rows + 128] = jnp.broadcast_to(query_sq[mine], (pairs_mine, 128))
-        message_ref[pairs_mine : pairs_mine + 1, rows : rows + 128] = jnp.zeros((1, 128), jnp.float32)
+        message_ref[:, 0:rows] = dots[mine]
+        message_ref[:, rows : rows + chunk] = jnp.zeros((pairs_mine, chunk), jnp.float32)
+        for row in range(rows // chunk):
+            message_ref[row : row + 1, rows : rows + chunk] = norm_ref[:, row * chunk : (row + 1) * chunk]
+        message_ref[:, rows + chunk :] = jnp.broadcast_to(query_sq[mine], (pairs_mine, 128))
 
 
 def dots(signs, partials, slab, bank_part, tp_count):
     pair_count = signs.shape[0]
     rows, cols = slab.shape
-    message = jax.ShapeDtypeStruct((pair_count // tp_count + 1, rows + 128), jnp.float32)
+    pairs_mine = pair_count // tp_count
+    message = jax.ShapeDtypeStruct(
+        (pairs_mine, rows + norm_chunk(rows, pairs_mine) + 128), jnp.float32
+    )
     return pl.pallas_call(
         dots_kernel,
         out_shape=[message] * tp_count,
@@ -257,14 +276,16 @@
     for got_ref in got_refs:
         total = total + got_ref[...]
     pairs, rows = out_ref.shape
-    bank_scale = lax.rsqrt(total[pairs : pairs + 1, 0:rows] + epsilon)
-    query_scale = lax.rsqrt(total[0:pairs, rows : rows + 1] + epsilon)
-    out_ref[...] = total[0:pairs, 0:rows] * scale * query_scale * bank_scale
-
-
-def scores(messages, scale):
-    pairs = messages[0].shape[0] - 1
-    rows = messages[0].shape[1] - 128
+    chunk = norm_chunk(rows, pairs)
+    query_scale = scale * lax.rsqrt(total[:, rows + chunk : rows + chunk + 1] + epsilon)
+    bank_scale = lax.rsqrt(total[:, rows : rows + chunk] + epsilon)
+    for row in range(rows // chunk):
+        span = slice(row * chunk, (row + 1) * chunk)
+        out_ref[:, span] = total[:, span] * query_scale * bank_scale[row : row + 1, :]
+
+
+def scores(messages, rows, scale):
+    pairs = messages[0].shape[0]
     return pl.pallas_call(
         functools.partial(scores_kernel, scale),
         out_shape=jax.ShapeDtypeStruct((pairs, rows), jnp.float32),
@@ -284,15 +305,20 @@
     out_got = lax.ppermute(out_away, "tp", flip(1))
     out_chip = add(out_keep(proj_held, rows_held), out_got, 4)
     out_other = lax.ppermute(out_chip, "tp", flip(2))
-    in_away, in_keep = in_factors(proj_in, hidden, out_chip)
+    in_away = in_factor(proj_in, hidden, out_chip, 1)
+    in_keep = in_factor(proj_in, hidden, in_away, 0)
     in_got = lax.ppermute(in_away, "tp", flip(1))
     out_full = add(out_chip, out_other, 4 * 10**9)
     bank_part = norms(bank_slab, in_away)
-    outgoing = outer(live, in_keep, in_got, out_full, bank_part, bank_count * tp_count)
-    partials = lax.all_to_all(outgoing, ("bank", "tp"), 0, 0, tiled=True)
+    outgoing = outer(
+        live, in_keep, in_got, out_full, bank_part, [device % 4 for device in exchange_order(bank_count)]
+    )
+    partials = lax.all_to_all(
+        outgoing, ("bank", "tp"), 0, 0, tiled=True, axis_index_groups=[exchange_order(bank_count)]
+    )
     messages = dots(signs, partials, bank_slab, bank_part, tp_count)
-    got = [messages[0]] + [lax.ppermute(messages[step], "tp", flip(step)) for step in range(1, 4)]
-    return scores(got, float(rank))
+    got = [messages[0]] + [lax.ppermute(messages[step], "tp", flip(step)) for step in (2, 3, 1)]
+    return scores(got, bank_slab.shape[0], float(rank))
 
 
 def solution(mesh):

time: 30.1 us -> 29.4 us (0.977)
  blocking collectives: 14.1 us -> 13.1 us
  starting transfers between devices: 5.38 us -> 5.74 us
  waiting for transfers between devices: 3.77 us -> 3.43 us
    all_to_all x1, blocking collectives: 14.1 us -> 13.1 us  [per_device(): lax.all_to_all(outgoing, ('bank', 'tp'), 0, 0, tiled=True, axis_index_gro...]
    ppermute x3, starting transfers between devices: 1.88 us -> 2.24 us  [per_device(): lax.ppermute(messages[step], 'tp', flip(step))]
    pallas_call x2 -> x3, Pallas kernels: 2.45 us -> 2.66 us  [the longest x2 2.31 us: in_factor(): pl.pallas_call(functools.partial(in_kernel, swap), out_shape=jax.ShapeDty...]
  transfers between devices with their start and end apart: 6 -> 6, of which waited for: 3 -> 4; matrix products, arithmetic and copies ran while one was open for 0% -> 0% of each run, Pallas kernels for 10% -> 11%
where the time goes in v5:
time: 29.4 us; the launch traced here: 29.2 us
  blocking collectives  13.1 us (45%)
  Pallas kernels  6.82 us (23%)
  starting transfers between devices  5.74 us (20%)
  waiting for transfers between devices  3.43 us (12%)
    all_to_all x1, blocking collectives, per_device(): lax.all_to_all(outgoing, ('bank', 'tp'), 0, 0, tiled=True, axis_index_gro...  13.1 us
    ppermute x1, starting transfers between devices, per_device(): out_other = lax.ppermute(out_chip, 'tp', flip(2))  2.91 us
    pallas_call x2, Pallas kernels, in_factor(): pl.pallas_call(functools.partial(in_kernel, swap), out_shape=jax.ShapeDty...  2.31 us
    ppermute x3, starting transfers between devices, per_device(): lax.ppermute(messages[step], 'tp', flip(step))  2.24 us
    ppermute x3, waiting for transfers between devices, per_device(): lax.ppermute(messages[step], 'tp', flip(step))  1.98 us
    pallas_call x1, Pallas kernels, out_send(): pl.pallas_call(functools.partial(out_send_kernel, pair_count // tp_count)...  1.74 us
    ppermute x1, waiting for transfers between devices, per_device(): out_other = lax.ppermute(out_chip, 'tp', flip(2))  0.92 us
    pallas_call x1, Pallas kernels, dots(): pl.pallas_call(dots_kernel, out_shape=[message] * tp_count, in_specs=[VME...  0.77 us
  transfers between devices with their start and end apart: 6, of which 4 were waited for; matrix products, arithmetic and copies ran while one was open for 0% of the time, Pallas kernels for 11%

profile of v5, /device:TPU:0, one launch (start us, length us, event | category | flops | bytes accessed | tf_op | source)
XLA Modules:
  0.0 29.2 jit_solution(7542024040527155208)
XLA Ops:
  0.0 1.7 %shard_map.73 = (f32[64,512]{1,0:T(8,128)S(1)}, bf16[64,1024]{1,0:T(8,128)(2,1)S(1)}, bf16[512,1024]{1,0:T(8,128)(2,1)S(1)}, f32[1,512]{1,0:T(1,128)S(1)}, f32[8,32]{1,0:T(8,128)S(1)}) custom-call(bf16[64,1024]{1,0:T(8,128)(2,1)} %proj_ref.3, bf16[2,512,1024]{2,1,0:T(8,128)(2,1)} %rows_ref.3, s32[2]{0:T(128)} %lengths_ref.1, s32[16]{0:T(128)} %perm_ref.1), custom_call_target="tpu_custom_call" | custom-call | flops 134217728 | bytes 2097152 | tf_op jit(solution)/shard_map/pallas_call | solution.py:83
  1.7 0.5 %collective-permute-start = (f32[64,512]{1,0:T(8,128)S(1)}, f32[64,512]{1,0:T(8,128)S(1)}, u32[]{:S(2)}, u32[]{:S(2)}) collective-permute-start(f32[64,512]{1,0:T(8,128)S(1)} %get-tuple-element.18), channel_id=1, source_target_pairs={{0,1},{1,0},{2,3},{3,2},{4,5},{5,4},{6,7},{7,6},{8,9},{9,8},{10,11... | collective-permute-start | bytes 393224 | tf_op jit(solution)/shard_map/ppermute | solution.py:305
  2.3 0.0 slice-start
  2.3 0.0 slice-start.1
  2.3 0.0 copy-start.1
  2.3 0.5 %shard_map.74.left_ref = f32[64,512]{1,0:T(8,128)S(1)} custom-call(bf16[64,1024]{1,0:T(8,128)(2,1)S(1)} %get-tuple-element.16.proj_ref, bf16[512,1024]{1,0:T(8,128)(2,1)S(1)} %get-tuple-element.17.rows_ref), custom_call_target="tpu_custom_call" | custom-call | flops 4000000000 | bytes 1048576 | tf_op jit(solution)/shard_map/pallas_call | solution.py:114
  2.7 0.5 %collective-permute-done.right_ref = f32[64,512]{1,0:T(8,128)S(1)} collective-permute-done((f32[64,512]{1,0:T(8,128)S(1)}, f32[64,512]{1,0:T(8,128)S(1)}, u32[]{:S(2)}, u32[]{:S(2)}) %collective-permute-start) | collective-permute-done | bytes 131104 | tf_op jit(solution)/shard_map/ppermute | solution.py:305
  3.3 0.0 copy-start
  3.3 2.9 %collective-permute-start.2 = (f32[64,512]{1,0:T(8,128)S(1)}, f32[64,512]{1,0:T(8,128)S(1)}, u32[]{:S(2)}, u32[]{:S(2)}) collective-permute-start(f32[64,512]{1,0:T(8,128)S(1)} %shard_map.75.after_ref.left_ref), channel_id=1, source_target_pairs={{0,2},{1,3},{2,0},{3,1},{4,6},{5,7},{6,4},{7,5},{8,10},{9,11},{10,... | collective-permute-start | bytes 393224 | tf_op jit(solution)/shard_map/ppermute | solution.py:307
  6.2 0.0 slice-done
  6.2 0.0 slice-done.1
  6.2 0.0 copy-done.1
  6.2 1.2 %shard_map.76.after_ref = f32[64,512]{1,0:T(8,128)S(1)} custom-call(bf16[64,3584]{1,0:T(8,128)(2,1)S(1)} %copy-done.1, bf16[2,512,3584]{2,1,0:T(8,128)(2,1)S(1)} %bitcast.1, f32[64,512]{1,0:T(8,128)S(1)} %shard_map.75.after_ref.left_ref), custom_call_target="tpu_custom_call" | custom-call | flops 469762048 | bytes 3670016 | tf_op jit(solution)/shard_map/pallas_call | solution.py:151
  7.4 0.1 collective-permute-start.1
  7.4 0.0 copy-done
  7.4 0.5 %shard_map.79.after_ref.norm_ref = f32[1,1024]{1,0:T(1,128)S(1)} custom-call(bf16[1024,1024]{1,0:T(8,128)(2,1)S(1)} %copy-done, f32[64,512]{1,0:T(8,128)S(1)} %shard_map.76.after_ref), custom_call_target="tpu_custom_call" | custom-call | flops 2097152 | bytes 2097152 | tf_op jit(solution)/shard_map/pallas_call | solution.py:208
  7.9 1.2 %shard_map.77.in_keep_ref = f32[64,512]{1,0:T(8,128)S(1)} custom-call(bf16[64,3584]{1,0:T(8,128)(2,1)S(1)} %copy-done.1, bf16[2,512,3584]{2,1,0:T(8,128)(2,1)S(1)} %bitcast.1, f32[64,512]{1,0:T(8,128)S(1)} %shard_map.76.after_ref), custom_call_target="tpu_custom_call" | custom-call | flops 469762048 | bytes 3670016 | tf_op jit(solution)/shard_map/pallas_call | solution.py:151
  9.1 0.9 %collective-permute-done.2.right_ref = f32[64,512]{1,0:T(8,128)S(1)} collective-permute-done((f32[64,512]{1,0:T(8,128)S(1)}, f32[64,512]{1,0:T(8,128)S(1)}, u32[]{:S(2)}, u32[]{:S(2)}) %collective-permute-start.2) | collective-permute-done | bytes 131104 | tf_op jit(solution)/shard_map/ppermute | solution.py:307
  10.0 0.0 collective-permute-done.1.in_got_ref
  10.0 0.3 %shard_map.80 = f32[32,8,128]{2,1,0:T(8,128)S(1)} custom-call(f32[1,512]{1,0:T(1,128)S(1)} %get-tuple-element.15.live_ref, f32[64,512]{1,0:T(8,128)S(1)} %shard_map.77.in_keep_ref, f32[64,512]{1,0:T(8,128)S(1)} %collective-permute-done.1.in_got_ref, f32[64,512]{1,0:T(8,128)S(1)} %shard_map.78.out_full_ref, f32[1,1024]{1,0:T(1,128)S(1)} %shard_map.79.after_ref.norm_ref), custom_call_target="tpu_custom_call" | custom-call | flops 25165824 | bytes 131072 | tf_op jit(solution)/shard_map/pallas_call | solution.py:183
  10.4 13.1 %all_to_all.5.partials_ref = f32[32,8,128]{2,1,0:T(8,128)S(1)} all-to-all(f32[32,8,128]{2,1,0:T(8,128)S(1)} %shard_map.80), channel_id=1, replica_groups={{24,16,8,0,25,17,9,1,28,20,12,4,29,21,13,5,26,18,10,2,27,19,11,3,30,22,..., dimensions={0} | all-to-all | bytes 262144 | tf_op jit(solution)/shard_map/all_to_all | solution.py:316
  23.5 0.8 %shard_map.81 = (f32[2,1664]{1,0:T(2,128)S(1)}, f32[2,1664]{1,0:T(2,128)S(1)}, f32[2,1664]{1,0:T(2,128)S(1)}, f32[2,1664]{1,0:T(2,128)S(1)}) custom-call(f32[8,32]{1,0:T(8,128)S(1)} %get-tuple-element.14.signs_ref, f32[32,8,128]{2,1,0:T(8,128)S(1)} %all_to_all.5.partials_ref, bf16[1024,1024]{1,0:T(8,128)(2,1)S(1)} %copy-done, ...), custom_call_target="tpu_custom_call" | custom-call | flops 16777216 | bytes 2097152 | tf_op jit(solution)/shard_map/pallas_call | solution.py:261
  24.3 1.1 %collective-permute-start.3 = (f32[2,1664]{1,0:T(2,128)S(1)}, f32[2,1664]{1,0:T(2,128)S(1)}, u32[]{:S(2)}, u32[]{:S(2)}) collective-permute-start(f32[2,1664]{1,0:T(2,128)S(1)} %get-tuple-element.20), channel_id=1, source_target_pairs={{0,2},{1,3},{2,0},{3,1},{4,6},{5,7},{6,4},{7,5},{8,10},{9,11},{10,... | collective-permute-start | bytes 39944 | tf_op jit(solution)/shard_map/ppermute | solution.py:320
  25.4 1.1 %collective-permute-start.4 = (f32[2,1664]{1,0:T(2,128)S(1)}, f32[2,1664]{1,0:T(2,128)S(1)}, u32[]{:S(2)}, u32[]{:S(2)}) collective-permute-start(f32[2,1664]{1,0:T(2,128)S(1)} %get-tuple-element.21), channel_id=1, source_target_pairs={{0,3},{1,2},{2,1},{3,0},{4,7},{5,6},{6,5},{7,4},{8,11},{9,10},{10,... | collective-permute-start | bytes 39944 | tf_op jit(solution)/shard_map/ppermute | solution.py:320
  26.5 0.0 collective-permute-start.5
  26.5 1.5 %collective-permute-done.3.refs_0_ = f32[2,1664]{1,0:T(2,128)S(1)} collective-permute-done((f32[2,1664]{1,0:T(2,128)S(1)}, f32[2,1664]{1,0:T(2,128)S(1)}, u32[]{:S(2)}, u32[]{:S(2)}) %collective-permute-start.3) | collective-permute-done | bytes 13344 | tf_op jit(solution)/shard_map/ppermute | solution.py:320
  28.1 0.5 %collective-permute-done.4.refs_1_ = f32[2,1664]{1,0:T(2,128)S(1)} collective-permute-done((f32[2,1664]{1,0:T(2,128)S(1)}, f32[2,1664]{1,0:T(2,128)S(1)}, u32[]{:S(2)}, u32[]{:S(2)}) %collective-permute-start.4) | collective-permute-done | bytes 13344 | tf_op jit(solution)/shard_map/ppermute | solution.py:320
  28.5 0.0 collective-permute-done.5.refs_2_
  28.5 0.7 %shard_map.82 = f32[2,1024]{1,0:T(2,128)} custom-call(f32[2,1664]{1,0:T(2,128)S(1)} %get-tuple-element.19.own_ref, f32[2,1664]{1,0:T(2,128)S(1)} %collective-permute-done.3.refs_0_, f32[2,1664]{1,0:T(2,128)S(1)} %collective-permute-done.4.refs_1_, f32[2,1664]{1,0:T(2,128)S(1)} %collective-permute-done.5.refs_2_), custom_call_target="tpu_custom_call" | custom-call | tf_op jit(solution)/shard_map/pallas_call | solution.py:289
  (3 shorter events, 0.0 us)
Async XLA Ops:
  1.7 1.5 %collective-permute-start = (f32[64,512]{1,0:T(8,128)S(1)}, f32[64,512]{1,0:T(8,128)S(1)}, u32[]{:S(2)}, u32[]{:S(2)}) collective-permute-start(f32[64,512]{1,0:T(8,128)S(1)} %get-tuple-element.18), channel_id=1, source_target_pairs={{0,1},{1,0},{2,3},{3,2},{4,5},{5,4},{6,7},{7,6},{8,9},{9,8},{10,11... | collective-permute-start | bytes 393224 | tf_op jit(solution)/shard_map/ppermute | solution.py:305
  2.3 3.9 %slice-start = ((s8[7340032]{0:T(1024)(128)(4,1)}), s8[4194304]{0:T(1024)(128)(4,1)S(1)}, s32[]{:S(2)}) async-start(s8[7340032]{0:T(1024)(128)(4,1)} %bitcast), calls=%async_computation.1 | async-start | bytes 8388608
  2.3 3.9 %slice-start.1 = ((s8[7340032]{0:T(1024)(128)(4,1)}), s8[3145728]{0:T(1024)(128)(4,1)S(1)}, s32[]{:S(2)}) async-start(s8[7340032]{0:T(1024)(128)(4,1)} %bitcast), calls=%async_computation.2 | async-start | bytes 6291456
  2.3 3.9 %copy-start.1 = (bf16[64,3584]{1,0:T(8,128)(2,1)S(1)}, bf16[64,3584]{1,0:T(8,128)(2,1)}, u32[]{:S(2)}) copy-start(bf16[64,3584]{1,0:T(8,128)(2,1)} %proj_ref.5) | copy-start | bytes 1376260
  3.3 4.2 %copy-start = (bf16[1024,1024]{1,0:T(8,128)(2,1)S(1)}, bf16[1024,1024]{1,0:T(8,128)(2,1)}, u32[]{:S(2)}) copy-start(bf16[1024,1024]{1,0:T(8,128)(2,1)} %slab_ref.3) | copy-start | bytes 6291460
  3.3 6.7 %collective-permute-start.2 = (f32[64,512]{1,0:T(8,128)S(1)}, f32[64,512]{1,0:T(8,128)S(1)}, u32[]{:S(2)}, u32[]{:S(2)}) collective-permute-start(f32[64,512]{1,0:T(8,128)S(1)} %shard_map.75.after_ref.left_ref), channel_id=1, source_target_pairs={{0,2},{1,3},{2,0},{3,1},{4,6},{5,7},{6,4},{7,5},{8,10},{9,11},{10,... | collective-permute-start | bytes 393224 | tf_op jit(solution)/shard_map/ppermute | solution.py:307
  7.4 2.7 %collective-permute-start.1 = (f32[64,512]{1,0:T(8,128)S(1)}, f32[64,512]{1,0:T(8,128)S(1)}, u32[]{:S(2)}, u32[]{:S(2)}) collective-permute-start(f32[64,512]{1,0:T(8,128)S(1)} %shard_map.76.after_ref), channel_id=1, source_target_pairs={{0,1},{1,0},{2,3},{3,2},{4,5},{5,4},{6,7},{7,6},{8,9},{9,8},{10,11... | collective-permute-start | bytes 393224 | tf_op jit(solution)/shard_map/ppermute | solution.py:310
  24.3 3.8 %collective-permute-start.3 = (f32[2,1664]{1,0:T(2,128)S(1)}, f32[2,1664]{1,0:T(2,128)S(1)}, u32[]{:S(2)}, u32[]{:S(2)}) collective-permute-start(f32[2,1664]{1,0:T(2,128)S(1)} %get-tuple-element.20), channel_id=1, source_target_pairs={{0,2},{1,3},{2,0},{3,1},{4,6},{5,7},{6,4},{7,5},{8,10},{9,11},{10,... | collective-permute-start | bytes 39944 | tf_op jit(solution)/shard_map/ppermute | solution.py:320
  25.4 3.1 %collective-permute-start.4 = (f32[2,1664]{1,0:T(2,128)S(1)}, f32[2,1664]{1,0:T(2,128)S(1)}, u32[]{:S(2)}, u32[]{:S(2)}) collective-permute-start(f32[2,1664]{1,0:T(2,128)S(1)} %get-tuple-element.21), channel_id=1, source_target_pairs={{0,3},{1,2},{2,1},{3,0},{4,7},{5,6},{6,5},{7,4},{8,11},{9,10},{10,... | collective-permute-start | bytes 39944 | tf_op jit(solution)/shard_map/ppermute | solution.py:320
  26.5 2.0 %collective-permute-start.5 = (f32[2,1664]{1,0:T(2,128)S(1)}, f32[2,1664]{1,0:T(2,128)S(1)}, u32[]{:S(2)}, u32[]{:S(2)}) collective-permute-start(f32[2,1664]{1,0:T(2,128)S(1)} %get-tuple-element.22), channel_id=1, source_target_pairs={{0,1},{1,0},{2,3},{3,2},{4,5},{5,4},{6,7},{7,6},{8,9},{9,8},{10,11... | collective-permute-start | bytes 39944 | tf_op jit(solution)/shard_map/ppermute | solution.py:320

commit v6 on v5

--- a/solution.py
+++ b/solution.py
@@ -32,6 +32,12 @@
         rows, proj, (((1,), (1,)), ((), ())), preferred_element_type=jnp.float32
     )
     out_ref[:, start : start + rows.shape[0]] = part.T
+
+
+def put_factor_rows(rows, proj, out_ref):
+    out_ref[...] = lax.dot_general(
+        proj, rows, (((1,), (1,)), ((), ())), preferred_element_type=jnp.float32
+    )
 
 
 def in_hbm(arr):
@@ -52,8 +58,8 @@
         pltpu.make_async_copy(proj_ref, proj_held, sems.at[3]),
         pltpu.make_async_copy(rows_ref.at[core], rows_held, sems.at[4]),
     ]
-    for copy in copies:
-        copy.start()
+    for at, copy in enumerate(copies):
+        copy.start(priority=1 if at == 4 else 0)
     copies[0].wait()
     copies[1].wait()
     position = lax.broadcasted_iota(jnp.int32, live_ref.shape, 1)
@@ -72,7 +78,7 @@
     signs_ref[...] = signs
     copies[2].wait()
     copies[3].wait()
-    put_factor(rows_buf[...], proj_held[...], send_ref, 0)
+    put_factor_rows(rows_buf[...], proj_held[...], send_ref)
     copies[4].wait()
 
 
@@ -105,7 +111,7 @@
 
 
 def out_keep_kernel(proj_ref, rows_ref, out_ref):
-    put_factor(rows_ref[...], proj_ref[...], out_ref, 0)
+    put_factor_rows(rows_ref[...], proj_ref[...], out_ref)
 
 
 def out_keep(proj, rows):
@@ -160,14 +166,20 @@
     )(proj, rows, after)
 
 
+def halves(wide):
+    high = wide.astype(jnp.bfloat16)
+    return high, (wide - high.astype(jnp.float32)).astype(jnp.bfloat16)
+
+
 def outer_kernel(shares, live_ref, in_keep_ref, in_got_ref, out_full_ref, after_ref, send_ref, grads_ref):
     rank = in_keep_ref.shape[0]
     masked = jnp.where(live_ref[...] > 0.0, in_keep_ref[...] + in_got_ref[...], 0.0)
+    in_high, in_low = halves(masked)
+    out_high, out_low = halves(out_full_ref[...])
     grads_ref[...] = lax.dot_general(
-        masked,
-        out_full_ref[...],
+        jnp.concatenate([in_high, in_high, in_low], axis=1),
+        jnp.concatenate([out_high, out_low, out_high], axis=1),
         (((1,), (1,)), ((), ())),
-        precision=lax.Precision.HIGHEST,
         preferred_element_type=jnp.float32,
     )
     half = rank // 2

time: 29.4 us -> 29.3 us (level)
  no operation moved by 1% of the time
where the time goes in v6:
time: 29.3 us; the launch traced here: 29.1 us
  blocking collectives  13.1 us (45%)
  Pallas kernels  6.72 us (23%)
  starting transfers between devices  5.74 us (20%)
  waiting for transfers between devices  3.44 us (12%)
    all_to_all x1, blocking collectives, per_device(): lax.all_to_all(outgoing, ('bank', 'tp'), 0, 0, tiled=True, axis_index_gro...  13.1 us
    ppermute x1, starting transfers between devices, per_device(): out_other = lax.ppermute(out_chip, 'tp', flip(2))  2.91 us
    pallas_call x2, Pallas kernels, in_factor(): pl.pallas_call(functools.partial(in_kernel, swap), out_shape=jax.ShapeDty...  2.32 us
    ppermute x3, starting transfers between devices, per_device(): lax.ppermute(messages[step], 'tp', flip(step))  2.24 us
    ppermute x3, waiting for transfers between devices, per_device(): lax.ppermute(messages[step], 'tp', flip(step))  1.98 us
    pallas_call x1, Pallas kernels, out_send(): pl.pallas_call(functools.partial(out_send_kernel, pair_count // tp_count)...  1.71 us
    ppermute x1, waiting for transfers between devices, per_device(): out_other = lax.ppermute(out_chip, 'tp', flip(2))  0.91 us
    pallas_call x1, Pallas kernels, dots(): pl.pallas_call(dots_kernel, out_shape=[message] * tp_count, in_specs=[VME...  0.77 us
  transfers between devices with their start and end apart: 6, of which 4 were waited for; matrix products, arithmetic and copies ran while one was open for 0% of the time, Pallas kernels for 11%

profile of v6, /device:TPU:0, one launch (start us, length us, event | category | flops | bytes accessed | tf_op | source)
XLA Modules:
  0.0 29.1 jit_solution(16303220448919059)
XLA Ops:
  0.0 1.7 %shard_map.73 = (f32[64,512]{1,0:T(8,128)S(1)}, bf16[64,1024]{1,0:T(8,128)(2,1)S(1)}, bf16[512,1024]{1,0:T(8,128)(2,1)S(1)}, f32[1,512]{1,0:T(1,128)S(1)}, f32[8,32]{1,0:T(8,128)S(1)}) custom-call(bf16[64,1024]{1,0:T(8,128)(2,1)} %proj_ref.3, bf16[2,512,1024]{2,1,0:T(8,128)(2,1)} %rows_ref.3, s32[2]{0:T(128)} %lengths_ref.1, s32[16]{0:T(128)} %perm_ref.1), custom_call_target="tpu_custom_call" | custom-call | flops 134217728 | bytes 2097152 | tf_op jit(solution)/shard_map/pallas_call | solution.py:89
  1.7 0.5 %collective-permute-start = (f32[64,512]{1,0:T(8,128)S(1)}, f32[64,512]{1,0:T(8,128)S(1)}, u32[]{:S(2)}, u32[]{:S(2)}) collective-permute-start(f32[64,512]{1,0:T(8,128)S(1)} %get-tuple-element.18), channel_id=1, source_target_pairs={{0,1},{1,0},{2,3},{3,2},{4,5},{5,4},{6,7},{7,6},{8,9},{9,8},{10,11... | collective-permute-start | bytes 393224 | tf_op jit(solution)/shard_map/ppermute | solution.py:317
  2.2 0.0 slice-start
  2.2 0.0 slice-start.1
  2.2 0.0 copy-start.1
  2.2 0.4 %shard_map.74.left_ref = f32[64,512]{1,0:T(8,128)S(1)} custom-call(bf16[64,1024]{1,0:T(8,128)(2,1)S(1)} %get-tuple-element.16.proj_ref, bf16[512,1024]{1,0:T(8,128)(2,1)S(1)} %get-tuple-element.17.rows_ref), custom_call_target="tpu_custom_call" | custom-call | flops 4000000000 | bytes 1048576 | tf_op jit(solution)/shard_map/pallas_call | solution.py:120
  2.7 0.5 %collective-permute-done.right_ref = f32[64,512]{1,0:T(8,128)S(1)} collective-permute-done((f32[64,512]{1,0:T(8,128)S(1)}, f32[64,512]{1,0:T(8,128)S(1)}, u32[]{:S(2)}, u32[]{:S(2)}) %collective-permute-start) | collective-permute-done | bytes 131104 | tf_op jit(solution)/shard_map/ppermute | solution.py:317
  3.2 0.0 copy-start
  3.3 2.9 %collective-permute-start.2 = (f32[64,512]{1,0:T(8,128)S(1)}, f32[64,512]{1,0:T(8,128)S(1)}, u32[]{:S(2)}, u32[]{:S(2)}) collective-permute-start(f32[64,512]{1,0:T(8,128)S(1)} %shard_map.75.after_ref.left_ref), channel_id=1, source_target_pairs={{0,2},{1,3},{2,0},{3,1},{4,6},{5,7},{6,4},{7,5},{8,10},{9,11},{10,... | collective-permute-start | bytes 393224 | tf_op jit(solution)/shard_map/ppermute | solution.py:319
  6.2 0.0 slice-done
  6.2 0.0 slice-done.1
  6.2 0.0 copy-done.1
  6.2 1.2 %shard_map.76.after_ref = f32[64,512]{1,0:T(8,128)S(1)} custom-call(bf16[64,3584]{1,0:T(8,128)(2,1)S(1)} %copy-done.1, bf16[2,512,3584]{2,1,0:T(8,128)(2,1)S(1)} %bitcast.1, f32[64,512]{1,0:T(8,128)S(1)} %shard_map.75.after_ref.left_ref), custom_call_target="tpu_custom_call" | custom-call | flops 469762048 | bytes 3670016 | tf_op jit(solution)/shard_map/pallas_call | solution.py:157
  7.3 0.1 collective-permute-start.1
  7.4 0.0 copy-done
  7.4 0.5 %shard_map.79.after_ref.norm_ref = f32[1,1024]{1,0:T(1,128)S(1)} custom-call(bf16[1024,1024]{1,0:T(8,128)(2,1)S(1)} %copy-done, f32[64,512]{1,0:T(8,128)S(1)} %shard_map.76.after_ref), custom_call_target="tpu_custom_call" | custom-call | flops 2097152 | bytes 2097152 | tf_op jit(solution)/shard_map/pallas_call | solution.py:220
  7.9 1.2 %shard_map.77.in_keep_ref = f32[64,512]{1,0:T(8,128)S(1)} custom-call(bf16[64,3584]{1,0:T(8,128)(2,1)S(1)} %copy-done.1, bf16[2,512,3584]{2,1,0:T(8,128)(2,1)S(1)} %bitcast.1, f32[64,512]{1,0:T(8,128)S(1)} %shard_map.76.after_ref), custom_call_target="tpu_custom_call" | custom-call | flops 469762048 | bytes 3670016 | tf_op jit(solution)/shard_map/pallas_call | solution.py:157
  9.1 0.9 %collective-permute-done.2.right_ref = f32[64,512]{1,0:T(8,128)S(1)} collective-permute-done((f32[64,512]{1,0:T(8,128)S(1)}, f32[64,512]{1,0:T(8,128)S(1)}, u32[]{:S(2)}, u32[]{:S(2)}) %collective-permute-start.2) | collective-permute-done | bytes 131104 | tf_op jit(solution)/shard_map/ppermute | solution.py:319
  10.0 0.0 collective-permute-done.1.in_got_ref
  10.0 0.3 shard_map.80
  10.3 13.1 %all_to_all.5.partials_ref = f32[32,8,128]{2,1,0:T(8,128)S(1)} all-to-all(f32[32,8,128]{2,1,0:T(8,128)S(1)} %shard_map.80), channel_id=1, replica_groups={{24,16,8,0,25,17,9,1,28,20,12,4,29,21,13,5,26,18,10,2,27,19,11,3,30,22,..., dimensions={0} | all-to-all | bytes 262144 | tf_op jit(solution)/shard_map/all_to_all | solution.py:328
  23.4 0.8 %shard_map.81 = (f32[2,1664]{1,0:T(2,128)S(1)}, f32[2,1664]{1,0:T(2,128)S(1)}, f32[2,1664]{1,0:T(2,128)S(1)}, f32[2,1664]{1,0:T(2,128)S(1)}) custom-call(f32[8,32]{1,0:T(8,128)S(1)} %get-tuple-element.14.signs_ref, f32[32,8,128]{2,1,0:T(8,128)S(1)} %all_to_all.5.partials_ref, bf16[1024,1024]{1,0:T(8,128)(2,1)S(1)} %copy-done, ...), custom_call_target="tpu_custom_call" | custom-call | flops 16777216 | bytes 2097152 | tf_op jit(solution)/shard_map/pallas_call | solution.py:273
  24.2 1.1 %collective-permute-start.3 = (f32[2,1664]{1,0:T(2,128)S(1)}, f32[2,1664]{1,0:T(2,128)S(1)}, u32[]{:S(2)}, u32[]{:S(2)}) collective-permute-start(f32[2,1664]{1,0:T(2,128)S(1)} %get-tuple-element.20), channel_id=1, source_target_pairs={{0,2},{1,3},{2,0},{3,1},{4,6},{5,7},{6,4},{7,5},{8,10},{9,11},{10,... | collective-permute-start | bytes 39944 | tf_op jit(solution)/shard_map/ppermute | solution.py:332
  25.3 1.1 %collective-permute-start.4 = (f32[2,1664]{1,0:T(2,128)S(1)}, f32[2,1664]{1,0:T(2,128)S(1)}, u32[]{:S(2)}, u32[]{:S(2)}) collective-permute-start(f32[2,1664]{1,0:T(2,128)S(1)} %get-tuple-element.21), channel_id=1, source_target_pairs={{0,3},{1,2},{2,1},{3,0},{4,7},{5,6},{6,5},{7,4},{8,11},{9,10},{10,... | collective-permute-start | bytes 39944 | tf_op jit(solution)/shard_map/ppermute | solution.py:332
  26.4 0.0 collective-permute-start.5
  26.4 1.5 %collective-permute-done.3.refs_0_ = f32[2,1664]{1,0:T(2,128)S(1)} collective-permute-done((f32[2,1664]{1,0:T(2,128)S(1)}, f32[2,1664]{1,0:T(2,128)S(1)}, u32[]{:S(2)}, u32[]{:S(2)}) %collective-permute-start.3) | collective-permute-done | bytes 13344 | tf_op jit(solution)/shard_map/ppermute | solution.py:332
  28.0 0.5 %collective-permute-done.4.refs_1_ = f32[2,1664]{1,0:T(2,128)S(1)} collective-permute-done((f32[2,1664]{1,0:T(2,128)S(1)}, f32[2,1664]{1,0:T(2,128)S(1)}, u32[]{:S(2)}, u32[]{:S(2)}) %collective-permute-start.4) | collective-permute-done | bytes 13344 | tf_op jit(solution)/shard_map/ppermute | solution.py:332
  28.4 0.0 collective-permute-done.5.refs_2_
  28.4 0.7 %shard_map.82 = f32[2,1024]{1,0:T(2,128)} custom-call(f32[2,1664]{1,0:T(2,128)S(1)} %get-tuple-element.19.own_ref, f32[2,1664]{1,0:T(2,128)S(1)} %collective-permute-done.3.refs_0_, f32[2,1664]{1,0:T(2,128)S(1)} %collective-permute-done.4.refs_1_, f32[2,1664]{1,0:T(2,128)S(1)} %collective-permute-done.5.refs_2_), custom_call_target="tpu_custom_call" | custom-call | tf_op jit(solution)/shard_map/pallas_call | solution.py:301
  (3 shorter events, 0.0 us)
Async XLA Ops:
  1.7 1.5 %collective-permute-start = (f32[64,512]{1,0:T(8,128)S(1)}, f32[64,512]{1,0:T(8,128)S(1)}, u32[]{:S(2)}, u32[]{:S(2)}) collective-permute-start(f32[64,512]{1,0:T(8,128)S(1)} %get-tuple-element.18), channel_id=1, source_target_pairs={{0,1},{1,0},{2,3},{3,2},{4,5},{5,4},{6,7},{7,6},{8,9},{9,8},{10,11... | collective-permute-start | bytes 393224 | tf_op jit(solution)/shard_map/ppermute | solution.py:317
  2.2 3.9 %slice-start = ((s8[7340032]{0:T(1024)(128)(4,1)}), s8[4194304]{0:T(1024)(128)(4,1)S(1)}, s32[]{:S(2)}) async-start(s8[7340032]{0:T(1024)(128)(4,1)} %bitcast), calls=%async_computation.1 | async-start | bytes 8388608
  2.2 3.9 %slice-start.1 = ((s8[7340032]{0:T(1024)(128)(4,1)}), s8[3145728]{0:T(1024)(128)(4,1)S(1)}, s32[]{:S(2)}) async-start(s8[7340032]{0:T(1024)(128)(4,1)} %bitcast), calls=%async_computation.2 | async-start | bytes 6291456
  2.2 3.9 %copy-start.1 = (bf16[64,3584]{1,0:T(8,128)(2,1)S(1)}, bf16[64,3584]{1,0:T(8,128)(2,1)}, u32[]{:S(2)}) copy-start(bf16[64,3584]{1,0:T(8,128)(2,1)} %proj_ref.5) | copy-start | bytes 1376260
  3.2 4.2 %copy-start = (bf16[1024,1024]{1,0:T(8,128)(2,1)S(1)}, bf16[1024,1024]{1,0:T(8,128)(2,1)}, u32[]{:S(2)}) copy-start(bf16[1024,1024]{1,0:T(8,128)(2,1)} %slab_ref.3) | copy-start | bytes 6291460
  3.3 6.7 %collective-permute-start.2 = (f32[64,512]{1,0:T(8,128)S(1)}, f32[64,512]{1,0:T(8,128)S(1)}, u32[]{:S(2)}, u32[]{:S(2)}) collective-permute-start(f32[64,512]{1,0:T(8,128)S(1)} %shard_map.75.after_ref.left_ref), channel_id=1, source_target_pairs={{0,2},{1,3},{2,0},{3,1},{4,6},{5,7},{6,4},{7,5},{8,10},{9,11},{10,... | collective-permute-start | bytes 393224 | tf_op jit(solution)/shard_map/ppermute | solution.py:319
  7.3 2.7 %collective-permute-start.1 = (f32[64,512]{1,0:T(8,128)S(1)}, f32[64,512]{1,0:T(8,128)S(1)}, u32[]{:S(2)}, u32[]{:S(2)}) collective-permute-start(f32[64,512]{1,0:T(8,128)S(1)} %shard_map.76.after_ref), channel_id=1, source_target_pairs={{0,1},{1,0},{2,3},{3,2},{4,5},{5,4},{6,7},{7,6},{8,9},{9,8},{10,11... | collective-permute-start | bytes 393224 | tf_op jit(solution)/shard_map/ppermute | solution.py:322
  24.2 3.8 %collective-permute-start.3 = (f32[2,1664]{1,0:T(2,128)S(1)}, f32[2,1664]{1,0:T(2,128)S(1)}, u32[]{:S(2)}, u32[]{:S(2)}) collective-permute-start(f32[2,1664]{1,0:T(2,128)S(1)} %get-tuple-element.20), channel_id=1, source_target_pairs={{0,2},{1,3},{2,0},{3,1},{4,6},{5,7},{6,4},{7,5},{8,10},{9,11},{10,... | collective-permute-start | bytes 39944 | tf_op jit(solution)/shard_map/ppermute | solution.py:332
  25.3 3.1 %collective-permute-start.4 = (f32[2,1664]{1,0:T(2,128)S(1)}, f32[2,1664]{1,0:T(2,128)S(1)}, u32[]{:S(2)}, u32[]{:S(2)}) collective-permute-start(f32[2,1664]{1,0:T(2,128)S(1)} %get-tuple-element.21), channel_id=1, source_target_pairs={{0,3},{1,2},{2,1},{3,0},{4,7},{5,6},{6,5},{7,4},{8,11},{9,10},{10,... | collective-permute-start | bytes 39944 | tf_op jit(solution)/shard_map/ppermute | solution.py:332
  26.4 2.0 %collective-permute-start.5 = (f32[2,1664]{1,0:T(2,128)S(1)}, f32[2,1664]{1,0:T(2,128)S(1)}, u32[]{:S(2)}, u32[]{:S(2)}) collective-permute-start(f32[2,1664]{1,0:T(2,128)S(1)} %get-tuple-element.22), channel_id=1, source_target_pairs={{0,1},{1,0},{2,3},{3,2},{4,5},{5,4},{6,7},{7,6},{8,9},{9,8},{10,11... | collective-permute-start | bytes 39944 | tf_op jit(solution)/shard_map/ppermute | solution.py:332

commit v7 on v6

--- a/solution.py
+++ b/solution.py
@@ -58,8 +58,8 @@
         pltpu.make_async_copy(proj_ref, proj_held, sems.at[3]),
         pltpu.make_async_copy(rows_ref.at[core], rows_held, sems.at[4]),
     ]
-    for at, copy in enumerate(copies):
-        copy.start(priority=1 if at == 4 else 0)
+    for at in (2, 3, 0, 1, 4):
+        copies[at].start(priority=1 if at == 4 else 0)
     copies[0].wait()
     copies[1].wait()
     position = lax.broadcasted_iota(jnp.int32, live_ref.shape, 1)

time: 29.3 us -> 29.3 us (level)
  no operation moved by 1% of the time
where the time goes in v7:
time: 29.3 us; the launch traced here: 29.1 us
  blocking collectives  13.1 us (45%)
  Pallas kernels  6.72 us (23%)
  starting transfers between devices  5.74 us (20%)
  waiting for transfers between devices  3.44 us (12%)
    all_to_all x1, blocking collectives, per_device(): lax.all_to_all(outgoing, ('bank', 'tp'), 0, 0, tiled=True, axis_index_gro...  13.1 us
    ppermute x1, starting transfers between devices, per_device(): out_other = lax.ppermute(out_chip, 'tp', flip(2))  2.91 us
    pallas_call x2, Pallas kernels, in_factor(): pl.pallas_call(functools.partial(in_kernel, swap), out_shape=jax.ShapeDty...  2.32 us
    ppermute x3, starting transfers between devices, per_device(): lax.ppermute(messages[step], 'tp', flip(step))  2.24 us
    ppermute x3, waiting for transfers between devices, per_device(): lax.ppermute(messages[step], 'tp', flip(step))  1.98 us
    pallas_call x1, Pallas kernels, out_send(): pl.pallas_call(functools.partial(out_send_kernel, pair_count // tp_count)...  1.71 us
    ppermute x1, waiting for transfers between devices, per_device(): out_other = lax.ppermute(out_chip, 'tp', flip(2))  0.91 us
    pallas_call x1, Pallas kernels, dots(): pl.pallas_call(dots_kernel, out_shape=[message] * tp_count, in_specs=[VME...  0.77 us
  transfers between devices with their start and end apart: 6, of which 4 were waited for; matrix products, arithmetic and copies ran while one was open for 0% of the time, Pallas kernels for 11%

profile of v7, /device:TPU:0, one launch (start us, length us, event | category | flops | bytes accessed | tf_op | source)
XLA Modules:
  0.0 29.1 jit_solution(14130249670820719394)
XLA Ops:
  0.0 1.7 %shard_map.73 = (f32[64,512]{1,0:T(8,128)S(1)}, bf16[64,1024]{1,0:T(8,128)(2,1)S(1)}, bf16[512,1024]{1,0:T(8,128)(2,1)S(1)}, f32[1,512]{1,0:T(1,128)S(1)}, f32[8,32]{1,0:T(8,128)S(1)}) custom-call(bf16[64,1024]{1,0:T(8,128)(2,1)} %proj_ref.3, bf16[2,512,1024]{2,1,0:T(8,128)(2,1)} %rows_ref.3, s32[2]{0:T(128)} %lengths_ref.1, s32[16]{0:T(128)} %perm_ref.1), custom_call_target="tpu_custom_call" | custom-call | flops 134217728 | bytes 2097152 | tf_op jit(solution)/shard_map/pallas_call | solution.py:89
  1.7 0.5 %collective-permute-start = (f32[64,512]{1,0:T(8,128)S(1)}, f32[64,512]{1,0:T(8,128)S(1)}, u32[]{:S(2)}, u32[]{:S(2)}) collective-permute-start(f32[64,512]{1,0:T(8,128)S(1)} %get-tuple-element.18), channel_id=1, source_target_pairs={{0,1},{1,0},{2,3},{3,2},{4,5},{5,4},{6,7},{7,6},{8,9},{9,8},{10,11... | collective-permute-start | bytes 393224 | tf_op jit(solution)/shard_map/ppermute | solution.py:317
  2.2 0.0 slice-start
  2.2 0.0 slice-start.1
  2.2 0.0 copy-start.1
  2.2 0.4 %shard_map.74.left_ref = f32[64,512]{1,0:T(8,128)S(1)} custom-call(bf16[64,1024]{1,0:T(8,128)(2,1)S(1)} %get-tuple-element.16.proj_ref, bf16[512,1024]{1,0:T(8,128)(2,1)S(1)} %get-tuple-element.17.rows_ref), custom_call_target="tpu_custom_call" | custom-call | flops 4000000000 | bytes 1048576 | tf_op jit(solution)/shard_map/pallas_call | solution.py:120
  2.7 0.5 %collective-permute-done.right_ref = f32[64,512]{1,0:T(8,128)S(1)} collective-permute-done((f32[64,512]{1,0:T(8,128)S(1)}, f32[64,512]{1,0:T(8,128)S(1)}, u32[]{:S(2)}, u32[]{:S(2)}) %collective-permute-start) | collective-permute-done | bytes 131104 | tf_op jit(solution)/shard_map/ppermute | solution.py:317
  3.2 0.0 copy-start
  3.3 2.9 %collective-permute-start.2 = (f32[64,512]{1,0:T(8,128)S(1)}, f32[64,512]{1,0:T(8,128)S(1)}, u32[]{:S(2)}, u32[]{:S(2)}) collective-permute-start(f32[64,512]{1,0:T(8,128)S(1)} %shard_map.75.after_ref.left_ref), channel_id=1, source_target_pairs={{0,2},{1,3},{2,0},{3,1},{4,6},{5,7},{6,4},{7,5},{8,10},{9,11},{10,... | collective-permute-start | bytes 393224 | tf_op jit(solution)/shard_map/ppermute | solution.py:319
  6.2 0.0 slice-done
  6.2 0.0 slice-done.1
  6.2 0.0 copy-done.1
  6.2 1.2 %shard_map.76.after_ref = f32[64,512]{1,0:T(8,128)S(1)} custom-call(bf16[64,3584]{1,0:T(8,128)(2,1)S(1)} %copy-done.1, bf16[2,512,3584]{2,1,0:T(8,128)(2,1)S(1)} %bitcast.1, f32[64,512]{1,0:T(8,128)S(1)} %shard_map.75.after_ref.left_ref), custom_call_target="tpu_custom_call" | custom-call | flops 469762048 | bytes 3670016 | tf_op jit(solution)/shard_map/pallas_call | solution.py:157
  7.3 0.1 collective-permute-start.1
  7.4 0.0 copy-done
  7.4 0.5 %shard_map.79.after_ref.norm_ref = f32[1,1024]{1,0:T(1,128)S(1)} custom-call(bf16[1024,1024]{1,0:T(8,128)(2,1)S(1)} %copy-done, f32[64,512]{1,0:T(8,128)S(1)} %shard_map.76.after_ref), custom_call_target="tpu_custom_call" | custom-call | flops 2097152 | bytes 2097152 | tf_op jit(solution)/shard_map/pallas_call | solution.py:220
  7.9 1.2 %shard_map.77.in_keep_ref = f32[64,512]{1,0:T(8,128)S(1)} custom-call(bf16[64,3584]{1,0:T(8,128)(2,1)S(1)} %copy-done.1, bf16[2,512,3584]{2,1,0:T(8,128)(2,1)S(1)} %bitcast.1, f32[64,512]{1,0:T(8,128)S(1)} %shard_map.76.after_ref), custom_call_target="tpu_custom_call" | custom-call | flops 469762048 | bytes 3670016 | tf_op jit(solution)/shard_map/pallas_call | solution.py:157
  9.1 0.9 %collective-permute-done.2.right_ref = f32[64,512]{1,0:T(8,128)S(1)} collective-permute-done((f32[64,512]{1,0:T(8,128)S(1)}, f32[64,512]{1,0:T(8,128)S(1)}, u32[]{:S(2)}, u32[]{:S(2)}) %collective-permute-start.2) | collective-permute-done | bytes 131104 | tf_op jit(solution)/shard_map/ppermute | solution.py:319
  10.0 0.0 collective-permute-done.1.in_got_ref
  10.0 0.3 shard_map.80
  10.3 13.1 %all_to_all.5.partials_ref = f32[32,8,128]{2,1,0:T(8,128)S(1)} all-to-all(f32[32,8,128]{2,1,0:T(8,128)S(1)} %shard_map.80), channel_id=1, replica_groups={{24,16,8,0,25,17,9,1,28,20,12,4,29,21,13,5,26,18,10,2,27,19,11,3,30,22,..., dimensions={0} | all-to-all | bytes 262144 | tf_op jit(solution)/shard_map/all_to_all | solution.py:328
  23.4 0.8 %shard_map.81 = (f32[2,1664]{1,0:T(2,128)S(1)}, f32[2,1664]{1,0:T(2,128)S(1)}, f32[2,1664]{1,0:T(2,128)S(1)}, f32[2,1664]{1,0:T(2,128)S(1)}) custom-call(f32[8,32]{1,0:T(8,128)S(1)} %get-tuple-element.14.signs_ref, f32[32,8,128]{2,1,0:T(8,128)S(1)} %all_to_all.5.partials_ref, bf16[1024,1024]{1,0:T(8,128)(2,1)S(1)} %copy-done, ...), custom_call_target="tpu_custom_call" | custom-call | flops 16777216 | bytes 2097152 | tf_op jit(solution)/shard_map/pallas_call | solution.py:273
  24.2 1.1 %collective-permute-start.3 = (f32[2,1664]{1,0:T(2,128)S(1)}, f32[2,1664]{1,0:T(2,128)S(1)}, u32[]{:S(2)}, u32[]{:S(2)}) collective-permute-start(f32[2,1664]{1,0:T(2,128)S(1)} %get-tuple-element.20), channel_id=1, source_target_pairs={{0,2},{1,3},{2,0},{3,1},{4,6},{5,7},{6,4},{7,5},{8,10},{9,11},{10,... | collective-permute-start | bytes 39944 | tf_op jit(solution)/shard_map/ppermute | solution.py:332
  25.3 1.1 %collective-permute-start.4 = (f32[2,1664]{1,0:T(2,128)S(1)}, f32[2,1664]{1,0:T(2,128)S(1)}, u32[]{:S(2)}, u32[]{:S(2)}) collective-permute-start(f32[2,1664]{1,0:T(2,128)S(1)} %get-tuple-element.21), channel_id=1, source_target_pairs={{0,3},{1,2},{2,1},{3,0},{4,7},{5,6},{6,5},{7,4},{8,11},{9,10},{10,... | collective-permute-start | bytes 39944 | tf_op jit(solution)/shard_map/ppermute | solution.py:332
  26.4 0.0 collective-permute-start.5
  26.4 1.5 %collective-permute-done.3.refs_0_ = f32[2,1664]{1,0:T(2,128)S(1)} collective-permute-done((f32[2,1664]{1,0:T(2,128)S(1)}, f32[2,1664]{1,0:T(2,128)S(1)}, u32[]{:S(2)}, u32[]{:S(2)}) %collective-permute-start.3) | collective-permute-done | bytes 13344 | tf_op jit(solution)/shard_map/ppermute | solution.py:332
  28.0 0.5 %collective-permute-done.4.refs_1_ = f32[2,1664]{1,0:T(2,128)S(1)} collective-permute-done((f32[2,1664]{1,0:T(2,128)S(1)}, f32[2,1664]{1,0:T(2,128)S(1)}, u32[]{:S(2)}, u32[]{:S(2)}) %collective-permute-start.4) | collective-permute-done | bytes 13344 | tf_op jit(solution)/shard_map/ppermute | solution.py:332
  28.4 0.0 collective-permute-done.5.refs_2_
  28.4 0.7 %shard_map.82 = f32[2,1024]{1,0:T(2,128)} custom-call(f32[2,1664]{1,0:T(2,128)S(1)} %get-tuple-element.19.own_ref, f32[2,1664]{1,0:T(2,128)S(1)} %collective-permute-done.3.refs_0_, f32[2,1664]{1,0:T(2,128)S(1)} %collective-permute-done.4.refs_1_, f32[2,1664]{1,0:T(2,128)S(1)} %collective-permute-done.5.refs_2_), custom_call_target="tpu_custom_call" | custom-call | tf_op jit(solution)/shard_map/pallas_call | solution.py:301
  (3 shorter events, 0.0 us)
Async XLA Ops:
  1.7 1.5 %collective-permute-start = (f32[64,512]{1,0:T(8,128)S(1)}, f32[64,512]{1,0:T(8,128)S(1)}, u32[]{:S(2)}, u32[]{:S(2)}) collective-permute-start(f32[64,512]{1,0:T(8,128)S(1)} %get-tuple-element.18), channel_id=1, source_target_pairs={{0,1},{1,0},{2,3},{3,2},{4,5},{5,4},{6,7},{7,6},{8,9},{9,8},{10,11... | collective-permute-start | bytes 393224 | tf_op jit(solution)/shard_map/ppermute | solution.py:317
  2.2 3.9 %slice-start = ((s8[7340032]{0:T(1024)(128)(4,1)}), s8[4194304]{0:T(1024)(128)(4,1)S(1)}, s32[]{:S(2)}) async-start(s8[7340032]{0:T(1024)(128)(4,1)} %bitcast), calls=%async_computation.1 | async-start | bytes 8388608
  2.2 3.9 %slice-start.1 = ((s8[7340032]{0:T(1024)(128)(4,1)}), s8[3145728]{0:T(1024)(128)(4,1)S(1)}, s32[]{:S(2)}) async-start(s8[7340032]{0:T(1024)(128)(4,1)} %bitcast), calls=%async_computation.2 | async-start | bytes 6291456
  2.2 3.9 %copy-start.1 = (bf16[64,3584]{1,0:T(8,128)(2,1)S(1)}, bf16[64,3584]{1,0:T(8,128)(2,1)}, u32[]{:S(2)}) copy-start(bf16[64,3584]{1,0:T(8,128)(2,1)} %proj_ref.5) | copy-start | bytes 1376260
  3.2 4.2 %copy-start = (bf16[1024,1024]{1,0:T(8,128)(2,1)S(1)}, bf16[1024,1024]{1,0:T(8,128)(2,1)}, u32[]{:S(2)}) copy-start(bf16[1024,1024]{1,0:T(8,128)(2,1)} %slab_ref.3) | copy-start | bytes 6291460
  3.3 6.7 %collective-permute-start.2 = (f32[64,512]{1,0:T(8,128)S(1)}, f32[64,512]{1,0:T(8,128)S(1)}, u32[]{:S(2)}, u32[]{:S(2)}) collective-permute-start(f32[64,512]{1,0:T(8,128)S(1)} %shard_map.75.after_ref.left_ref), channel_id=1, source_target_pairs={{0,2},{1,3},{2,0},{3,1},{4,6},{5,7},{6,4},{7,5},{8,10},{9,11},{10,... | collective-permute-start | bytes 393224 | tf_op jit(solution)/shard_map/ppermute | solution.py:319
  7.3 2.7 %collective-permute-start.1 = (f32[64,512]{1,0:T(8,128)S(1)}, f32[64,512]{1,0:T(8,128)S(1)}, u32[]{:S(2)}, u32[]{:S(2)}) collective-permute-start(f32[64,512]{1,0:T(8,128)S(1)} %shard_map.76.after_ref), channel_id=1, source_target_pairs={{0,1},{1,0},{2,3},{3,2},{4,5},{5,4},{6,7},{7,6},{8,9},{9,8},{10,11... | collective-permute-start | bytes 393224 | tf_op jit(solution)/shard_map/ppermute | solution.py:322
  24.2 3.8 %collective-permute-start.3 = (f32[2,1664]{1,0:T(2,128)S(1)}, f32[2,1664]{1,0:T(2,128)S(1)}, u32[]{:S(2)}, u32[]{:S(2)}) collective-permute-start(f32[2,1664]{1,0:T(2,128)S(1)} %get-tuple-element.20), channel_id=1, source_target_pairs={{0,2},{1,3},{2,0},{3,1},{4,6},{5,7},{6,4},{7,5},{8,10},{9,11},{10,... | collective-permute-start | bytes 39944 | tf_op jit(solution)/shard_map/ppermute | solution.py:332
  25.3 3.1 %collective-permute-start.4 = (f32[2,1664]{1,0:T(2,128)S(1)}, f32[2,1664]{1,0:T(2,128)S(1)}, u32[]{:S(2)}, u32[]{:S(2)}) collective-permute-start(f32[2,1664]{1,0:T(2,128)S(1)} %get-tuple-element.21), channel_id=1, source_target_pairs={{0,3},{1,2},{2,1},{3,0},{4,7},{5,6},{6,5},{7,4},{8,11},{9,10},{10,... | collective-permute-start | bytes 39944 | tf_op jit(solution)/shard_map/ppermute | solution.py:332
  26.4 2.0 %collective-permute-start.5 = (f32[2,1664]{1,0:T(2,128)S(1)}, f32[2,1664]{1,0:T(2,128)S(1)}, u32[]{:S(2)}, u32[]{:S(2)}) collective-permute-start(f32[2,1664]{1,0:T(2,128)S(1)} %get-tuple-element.22), channel_id=1, source_target_pairs={{0,1},{1,0},{2,3},{3,2},{4,5},{5,4},{6,7},{7,6},{8,9},{9,8},{10,11... | collective-permute-start | bytes 39944 | tf_op jit(solution)/shard_map/ppermute | solution.py:332
